TPU v7x, 128 devices: a whole 4x4x4 slice. The times are simulated.
128 devices in a mesh: rows: 16 (over y, x_lo, core), cols: 8 (over z, x_hi).
Axes of the slice: x: 4 (x_hi: 2, x_lo: 2; x = x_hi * 2 + x_lo), y: 4, z: 4, core: 2. Of those that a mesh axis runs over, the one named last changes fastest.
Arguments:
- latents: bfloat16 [1, 256, 256, 192], P(None, 'rows', 'cols'), may hold values from -200 to 200
- actions: int32 [1, 16], replicated, may hold values from 0 to 255
- action_table: bfloat16 [256, 192], replicated, may hold values from -16 to 16
- offsets: int32 [2, 2], replicated, may hold values from 1 to 8, as said below
- fine_gain: float32 [192], replicated, may hold values from 0.1 to 1.9
- fine_qkv: bfloat16 [192, 576], replicated, may hold values from -0.4375 to 0.4375
- fine_bias: float32 [6, 64, 64], replicated, may hold values from -3 to 320
- fine_proj: bfloat16 [192, 192], replicated, may hold values from -0.4375 to 0.4375
- merge_gain: float32 [768], replicated, may hold values from 0.1 to 1.9
- merge_weight: bfloat16 [768, 384], replicated, may hold values from -0.21875 to 0.21875
- coarse_gain: float32 [384], replicated, may hold values from 0.1 to 1.9
- coarse_qkv: bfloat16 [384, 1152], replicated, may hold values from -0.3125 to 0.3125
- coarse_bias: float32 [12, 64, 64], replicated, may hold values from -3 to 320
- coarse_proj: bfloat16 [384, 384], replicated, may hold values from -0.3125 to 0.3125
- head_weight: bfloat16 [384, 768], replicated, may hold values from -0.3125 to 0.3125
- cotangent: bfloat16 [1, 256, 256, 192], P(None, 'rows', 'cols'), may hold values from -0.046875 to 0.046875
Outputs:
- prediction: bfloat16 [1, 256, 256, 192], P(None, 'rows', 'cols')
- grad_fineqkv: float32 [192, 576], replicated
- grad_fineproj: float32 [192, 192], replicated
- grad_merge: float32 [768, 384], replicated
- grad_coarseqkv: float32 [384, 1152], replicated
- grad_coarseproj: float32 [384, 384], replicated
- grad_head: float32 [384, 768], replicated
Inputs may be any that keep to these rules, and one draw needn't show every extreme that they name: offsets[0] is the shift of the fine map and offsets[1] that of the merged map, in cells of that map; at least one entry equals 8.
All inputs are finite; a program needn't handle non-finite values.
Results may differ from a plain program's by a relative error of at most 0.02.
Values may be sent and summed in bfloat16 or wider, within the bound.
A program may use at most 128 MiB of HBM per device.

v0:
```python
import jax
import jax.numpy as jnp
from jax import lax
from jax.experimental import pallas as pl
from jax.experimental.pallas import tpu as pltpu
from jax.sharding import PartitionSpec as P

MESH = pl.DeviceIdType.MESH
BF = jnp.bfloat16
F32 = jnp.float32
EPS = 1e-05
SCALE = 32 ** (-0.5)
FINE_GROUPS = ((0, 128, 4), (128, 64, 2))
COARSE_GROUPS = ((0, 128, 4), (128, 128, 4), (256, 128, 4))
UNITS = (224, 224, 160, 96)
USED = (216, 216, 144, 72)
ORDERS = (("x", "y", "z"), ("y", "z", "x"), ("z", "x", "y"), ("x", "y", "z"))


def mm(a, b):
    return lax.dot_general(a, b, (((1,), (0,)), ((), ())), preferred_element_type=F32)


def mm_nt(a, b):
    return lax.dot_general(a, b, (((1,), (1,)), ((), ())), preferred_element_type=F32)


def mm_tn(a, b):
    return lax.dot_general(a, b, (((0,), (0,)), ((), ())), preferred_element_type=F32)


def norm(x):
    centred = x - jnp.mean(x, axis=-1, keepdims=True)
    inverse = lax.rsqrt(jnp.mean(centred * centred, axis=-1, keepdims=True) + EPS)
    return centred * inverse, inverse


def norm_back(upstream, unit, inverse, gain):
    e = upstream * gain
    return inverse * (
        e - jnp.mean(e, axis=-1, keepdims=True) - unit * jnp.mean(e * unit, axis=-1, keepdims=True)
    )


def head_masks(width, heads, dtype):
    lane = lax.broadcasted_iota(jnp.int32, (1, width), 1) // 32
    return [jnp.where(lane == h, 1.0, 0.0).astype(dtype) for h in range(heads)]


def spread(x, masks):
    return jnp.concatenate([x * m for m in masks], axis=0)


def fold(x, masks):
    total = x[:64] * masks[0]
    for h in range(1, len(masks)):
        total = total + x[64 * h : 64 * h + 64] * masks[h]
    return total


def probabilities(q, k, bias, masks):
    s = mm_nt(k, spread(q, masks)) * SCALE + bias
    e = jnp.exp(s - jnp.max(s, axis=0, keepdims=True))
    return e / jnp.sum(e, axis=0, keepdims=True)


def select(rows_out, cols_in, picks):
    x = lax.broadcasted_iota(jnp.int32, (rows_out, cols_in), 0)
    u = lax.broadcasted_iota(jnp.int32, (rows_out, cols_in), 1)
    return jnp.where(picks(x) == u, 1.0, 0.0).astype(F32).astype(BF)


def folded_place(u):
    v = u & 15
    return (u - v) + (v & 1) * 8 + (v >> 1)


def true_place(p):
    v = p & 15
    return (p - v) + (v & 7) * 2 + (v >> 3)


def units(x):
    return x.reshape(x.shape[0] // 16, 16, 128)


class Net:
    def __init__(self, send, recv):
        self.r = lax.axis_index("rows")
        self.c = lax.axis_index("cols")
        r, c = self.r, self.c
        self.core = lax.rem(r, 2)
        xlo = lax.rem(r // 2, 2)
        self.y = r // 4
        self.z = c // 2
        xhi = lax.rem(c, 2)
        self.x = xhi * 2 + xlo
        self.low = lax.rem(r, 4)
        self.xhi = xhi
        self.send, self.recv = send, recv
        self.count = 0
        self.copies = []

    def near(self, dr, dc):
        return (lax.rem(self.r + dr + 16, 16), lax.rem(self.c + dc + 8, 8))

    def place(self, axis):
        return {"x": self.x, "y": self.y, "z": self.z}[axis]

    def peer(self, axis, index):
        if axis == "y":
            return (index * 4 + self.low, self.c)
        if axis == "z":
            return (self.r, index * 2 + self.xhi)
        return (self.y * 4 + lax.rem(index, 2) * 2 + self.core, self.z * 2 + index // 2)

    def sibling(self):
        return (self.r + 1 - 2 * self.core, self.c)

    def start(self, source, target, device):
        n = self.count
        self.count += 1
        copy = pltpu.make_async_remote_copy(
            src_ref=source,
            dst_ref=target,
            send_sem=self.send.at[n],
            recv_sem=self.recv.at[n],
            device_id=device,
            device_id_type=MESH,
        )
        copy.start()
        self.copies.append(copy)
        return copy

    def barrier(self):
        sem = pltpu.get_barrier_semaphore()
        others = [self.near(a, b) for a in (-1, 0, 1) for b in (-1, 0, 1) if (a, b) != (0, 0)]
        others.append(self.sibling())
        for axis in "xyz":
            others += [self.peer(axis, lax.rem(self.place(axis) + k, 4)) for k in (1, 2, 3)]
        for device in others:
            pl.semaphore_signal(sem, inc=1, device_id=device, device_id_type=MESH)
        pl.semaphore_wait(sem, len(others))


class Reduce:
    def __init__(self, net, order, terms, got_core, got_a, sum_a, got_b, sum_b, got_c, result):
        self.net, self.order = net, order
        self.terms, self.got_core, self.got_a, self.sum_a = terms, got_core, got_a, sum_a
        self.got_b, self.sum_b, self.got_c, self.result = got_b, sum_b, got_c, result
        self.n = terms.shape[0]
        self.stage = 0
        self.flight = []

    def step(self):
        getattr(self, "step%d" % self.stage)()
        self.stage += 1

    def finish(self):
        while self.stage < 8:
            self.step()

    def arrive(self):
        for copy in self.flight:
            copy.wait_recv()

    def step0(self):
        net, half = self.net, self.n // 2
        self.flight = [
            net.start(self.terms.at[pl.ds((1 - net.core) * half, half)], self.got_core, net.sibling())
        ]

    def step1(self):
        net, half, part = self.net, self.n // 2, self.n // 8
        self.arrive()
        own = self.terms[pl.ds(net.core * half, half)].astype(F32)
        self.sum_a[...] = (own + self.got_core[...].astype(F32)).astype(BF)
        me = net.place(self.order[0])
        self.flight = []
        for k in (1, 2, 3):
            to = lax.rem(me + k, 4)
            self.flight.append(
                net.start(
                    self.sum_a.at[pl.ds(to * part, part)],
                    self.got_a.at[k - 1],
                    net.peer(self.order[0], to),
                )
            )

    def step2(self):
        net, part, piece = self.net, self.n // 8, self.n // 32
        self.arrive()
        total = self.sum_a[pl.ds(net.place(self.order[0]) * part, part)].astype(F32)
        for k in range(3):
            total = total + self.got_a[k].astype(F32)
        self.sum_b[...] = total.astype(BF)
        me = net.place(self.order[1])
        self.flight = []
        for k in (1, 2, 3):
            to = lax.rem(me + k, 4)
            self.flight.append(
                net.start(
                    self.sum_b.at[pl.ds(to * piece, piece)],
                    self.got_b.at[k - 1],
                    net.peer(self.order[1], to),
                )
            )

    def step3(self):
        net, piece = self.net, self.n // 32
        self.arrive()
        total = self.sum_b[pl.ds(net.place(self.order[1]) * piece, piece)].astype(F32)
        for k in range(3):
            total = total + self.got_b[k].astype(F32)
        me = net.place(self.order[2])
        self.got_c[pl.ds(me, 1)] = total.astype(BF)[None]
        self.flight = []
        for k in (1, 2, 3):
            to = lax.rem(me + k, 4)
            self.flight.append(
                net.start(self.got_c.at[me], self.got_c.at[me], net.peer(self.order[2], to))
            )

    def slot(self, depth):
        net, n = self.net, self.n
        at = net.core * (n // 2)
        if depth > 0:
            at = at + net.place(self.order[0]) * (n // 8)
        if depth > 1:
            at = at + net.place(self.order[1]) * (n // 32)
        return self.result.at[pl.ds(at, n // (2, 8, 32)[depth])]

    def step4(self):
        net = self.net
        self.arrive()
        total = self.got_c[0].astype(F32)
        for k in (1, 2, 3):
            total = total + self.got_c[k].astype(F32)
        mine = self.slot(2)
        mine[...] = total.astype(BF)
        me = net.place(self.order[1])
        self.flight = [
            net.start(mine, mine, net.peer(self.order[1], lax.rem(me + k, 4))) for k in (1, 2, 3)
        ]

    def step5(self):
        net = self.net
        self.arrive()
        mine = self.slot(1)
        me = net.place(self.order[0])
        self.flight = [
            net.start(mine, mine, net.peer(self.order[0], lax.rem(me + k, 4))) for k in (1, 2, 3)
        ]

    def step6(self):
        net = self.net
        self.arrive()
        mine = self.slot(0)
        self.flight = [net.start(mine, mine, net.sibling())]

    def step7(self):
        self.arrive()


def to_map(x, rows, cols):
    wide = cols // 8
    out = []
    for i in range(rows):
        base = (i // 8) * wide
        out.append(
            jnp.concatenate(
                [x[(base + w) * 64 + (i % 8) * 8 :][:8] for w in range(wide)], axis=0
            )
        )
    return out


def to_windows(rows_list, cols):
    wide = cols // 8
    pieces = []
    for wr in range(len(rows_list) // 8):
        for w in range(wide):
            for i in range(8):
                pieces.append(rows_list[wr * 8 + i][8 * w : 8 * w + 8])
    return jnp.concatenate(pieces, axis=0)


def paired(rows_list):
    out = []
    for di in (0, 1):
        for dj in (0, 1):
            out.append(
                jnp.concatenate(
                    [
                        rows_list[2 * i + di][16 * w + 8 * dj :][:8]
                        for w in (0, 1)
                        for i in range(8)
                    ],
                    axis=0,
                )
            )
    return out


def unpaired(parts):
    rows_list = []
    for row in range(16):
        i, di = row // 2, row % 2
        rows_list.append(
            jnp.concatenate(
                [
                    parts[2 * di + dj][64 * w + 8 * i :][:8]
                    for w in (0, 1)
                    for dj in (0, 1)
                ],
                axis=0,
            )
        )
    return rows_list


def body(
    offsets, actions, table, fgain, fqkv, fbias, fproj, mgain, mweight, cgain, cqkv, cbias, cproj,
    hweight, lat_hbm, cot_hbm,
    pred, res0, res1, res2, res3,
    lat, cot, fine_ahead, head_back, grad_back,
    fprobs, cprobs,
    *rest,
):
    works = [rest[7 * g : 7 * g + 7] for g in range(4)]
    send, recv, local = rest[28:]
    results = (res0, res1, res2, res3)
    net = Net(send, recv)
    bundles = []
    for g in range(4):
        terms, got_core, got_a, sum_a, got_b, sum_b, got_c = works[g]
        bundles.append(
            Reduce(
                net, ORDERS[g], terms, got_core, got_a, sum_a, got_b, sum_b, got_c, results[g]
            )
        )

    a0, a1 = offsets[0, 0], offsets[0, 1]
    b0, b1 = 2 * offsets[1, 0], 2 * offsets[1, 1]
    d0, d1 = lax.rem(b0 - a0 + 8, 8), lax.rem(b1 - a1 + 8, 8)
    s0, s1 = b0 - d0, b1 - d1

    own_lat = pltpu.make_async_copy(
        lat_hbm.at[0], lat.at[pl.ds(8, 16), pl.ds(16, 32)], local.at[0]
    )
    own_cot = pltpu.make_async_copy(
        cot_hbm.at[0], cot.at[pl.ds(0, 16), pl.ds(0, 32)], local.at[1]
    )
    own_lat.start()
    own_cot.start()
    net.barrier()

    row_cut = {-1: (0, 16, 24), 0: (0, 16, 8), 1: (8, 8, 0)}
    col_cut = {-1: (0, 16, 48), 0: (0, 32, 16), 1: (16, 16, 0)}
    lat_halo = []
    for dr, dc in ((-1, 0), (1, 0), (0, -1), (0, 1), (-1, -1), (-1, 1), (1, -1), (1, 1)):
        fr, nr, tr = row_cut[dr]
        fc, nc, tc = col_cut[dc]
        lat_halo.append(
            net.start(
                lat_hbm.at[0, pl.ds(fr, nr), pl.ds(fc, nc)],
                lat.at[pl.ds(tr, nr), pl.ds(tc, nc)],
                net.near(dr, dc),
            )
        )
    cot_halo = [
        net.start(cot_hbm.at[0], cot.at[pl.ds(16, 16), pl.ds(0, 32)], net.near(-1, 0)),
        net.start(
            cot_hbm.at[0, :, pl.ds(0, 16)], cot.at[pl.ds(0, 16), pl.ds(32, 16)], net.near(0, -1)
        ),
        net.start(
            cot_hbm.at[0, :, pl.ds(0, 16)], cot.at[pl.ds(16, 16), pl.ds(32, 16)], net.near(-1, -1)
        ),
    ]

    code = lax.broadcasted_iota(jnp.int32, (8, 256), 1)
    counts = jnp.zeros((8, 256), F32)
    for j in range(16):
        counts = counts + jnp.where(code == actions[0, j], 1.0, 0.0)
    condition = mm(counts.astype(BF), table[...])[:1] * (1.0 / 16.0)
    f_masks16 = [head_masks(w, h, BF) for _, w, h in FINE_GROUPS]
    f_masks32 = [head_masks(w, h, F32) for _, w, h in FINE_GROUPS]
    c_masks16 = [head_masks(w, h, BF) for _, w, h in COARSE_GROUPS]
    c_masks32 = [head_masks(w, h, F32) for _, w, h in COARSE_GROUPS]
    fb = fbias[...].reshape(384, 64).T
    cb = cbias[...].reshape(768, 64).T
    fw = [fqkv[:, 192 * i : 192 * i + 192] for i in range(3)]
    cw = [cqkv[:, 384 * i : 384 * i + 384] for i in range(3)]
    f_gain = fgain[...].reshape(1, 192)
    m_gain = mgain[...].reshape(1, 768)
    c_gain = cgain[...].reshape(1, 384)

    own_lat.wait()
    for copy in lat_halo:
        copy.wait_recv()
    pick = select(32, 64, lambda x: x + (s1 + 16))
    block = lat[pl.ds(8 + s0, 16)]
    residual = to_windows([mm(pick, block[i]) for i in range(16)], 32) + condition
    n1 = (norm(residual)[0] * f_gain).astype(BF)
    fq, fk, fv = (mm(n1, w).astype(BF) for w in fw)
    mixed = []
    for w in range(8):
        tokens = slice(64 * w, 64 * w + 64)
        line = []
        for g, (at, wide, heads) in enumerate(FINE_GROUPS):
            lanes = slice(at, at + wide)
            p = probabilities(
                fq[tokens, lanes], fk[tokens, lanes], fb[:, 64 * (at // 32) :][:, : 64 * heads],
                f_masks16[g],
            )
            fprobs[w, :, pl.ds(64 * (at // 32), 64 * heads)] = p
            line.append(fold(mm_tn(p.astype(BF), fv[tokens, lanes]), f_masks32[g]))
        mixed.append(jnp.concatenate(line, axis=1))
    f_mixed = jnp.concatenate(mixed, axis=0).astype(BF)
    attn = mm(f_mixed, fproj[...]).astype(BF)
    f_next = residual + attn.astype(F32)
    for i, row in enumerate(to_map(f_next, 16, 32)):
        fine_ahead[i, pl.ds(0, 32)] = row.astype(BF)
    ahead = [
        net.start(
            fine_ahead.at[pl.ds(0, 8), pl.ds(0, 32)], fine_ahead.at[pl.ds(16, 8), pl.ds(0, 32)],
            net.near(-1, 0),
        ),
        net.start(
            fine_ahead.at[pl.ds(0, 16), pl.ds(0, 16)], fine_ahead.at[pl.ds(0, 16), pl.ds(32, 16)],
            net.near(0, -1),
        ),
        net.start(
            fine_ahead.at[pl.ds(0, 8), pl.ds(0, 16)], fine_ahead.at[pl.ds(16, 8), pl.ds(32, 16)],
            net.near(-1, -1),
        ),
    ]

    own_cot.wait()
    for copy in cot_halo:
        copy.wait_recv()
    pick = select(32, 48, lambda x: true_place(x) + b1)
    block = cot[pl.ds(b0, 16)]
    grad_out = jnp.concatenate(paired([mm(pick, block[i]) for i in range(16)]), axis=1).astype(BF)
    grad_next = mm_nt(grad_out, hweight[...]).astype(BF)
    c_mixed_grad = mm_nt(grad_next, cproj[...]).astype(BF)

    for copy in ahead:
        copy.wait_recv()
    pick = select(32, 48, lambda x: true_place(x) + d1)
    block = fine_ahead[pl.ds(d0, 16)]
    merged = jnp.concatenate(paired([mm(pick, block[i]) for i in range(16)]), axis=1)
    m_unit, m_inverse = norm(merged)
    n2 = (m_unit * m_gain).astype(BF)
    c_residual = mm(n2, mweight[...]).astype(BF).astype(F32)
    c_unit, c_inverse = norm(c_residual)
    n3 = (c_unit * c_gain).astype(BF)
    cq, ck, cv = (mm(n3, w).astype(BF) for w in cw)
    mixed = []
    for w in range(2):
        tokens = slice(64 * w, 64 * w + 64)
        line = []
        for g, (at, wide, heads) in enumerate(COARSE_GROUPS):
            lanes = slice(at, at + wide)
            p = probabilities(
                cq[tokens, lanes], ck[tokens, lanes], cb[:, 64 * (at // 32) :][:, : 64 * heads],
                c_masks16[g],
            )
            cprobs[w, :, pl.ds(64 * (at // 32), 64 * heads)] = p
            line.append(fold(mm_tn(p.astype(BF), cv[tokens, lanes]), c_masks32[g]))
        mixed.append(jnp.concatenate(line, axis=1))
    c_mixed = jnp.concatenate(mixed, axis=0).astype(BF)
    c_attn = mm(c_mixed, cproj[...]).astype(BF)
    c_next = (c_residual + c_attn.astype(F32)).astype(BF)

    g_head = mm_tn(c_next, grad_out)
    for j in range(6):
        works[0][0][pl.ds(24 * j, 24)] = units(g_head[:, 128 * j : 128 * j + 128].astype(BF))
    g_cproj = mm_tn(c_mixed, grad_next)
    for j in range(3):
        works[0][0][pl.ds(144 + 24 * j, 24)] = units(
            g_cproj[:, 128 * j : 128 * j + 128].astype(BF)
        )
    works[0][0][pl.ds(216, 8)] = jnp.zeros((8, 16, 128), BF)
    bundles[0].step()

    head_out = mm(c_next, hweight[...])
    for i, row in enumerate(unpaired([head_out[:, 192 * t : 192 * t + 192] for t in range(4)])):
        head_back[16 + i, pl.ds(16, 32)] = row.astype(BF)
    back = [
        net.start(
            head_back.at[pl.ds(16, 16), pl.ds(16, 32)], head_back.at[pl.ds(0, 16), pl.ds(16, 32)],
            net.near(1, 0),
        ),
        net.start(
            head_back.at[pl.ds(16, 16), pl.ds(32, 16)], head_back.at[pl.ds(16, 16), pl.ds(0, 16)],
            net.near(0, 1),
        ),
        net.start(
            head_back.at[pl.ds(16, 16), pl.ds(32, 16)], head_back.at[pl.ds(0, 16), pl.ds(0, 16)],
            net.near(1, 1),
        ),
    ]

    def attention_back(probs, w, q, k, v, mixed_grad, groups, masks16, masks32):
        tokens = slice(64 * w, 64 * w + 64)
        dq, dk, dv = [], [], []
        for g, (at, wide, heads) in enumerate(groups):
            lanes = slice(at, at + wide)
            p = probs[w, :, pl.ds(64 * (at // 32), 64 * heads)]
            many_grad = spread(mixed_grad[tokens, lanes], masks16[g])
            wg = mm_nt(v[tokens, lanes], many_grad).astype(BF).astype(F32)
            sg = (p * (wg - jnp.sum(p * wg, axis=0, keepdims=True)) * SCALE).astype(BF)
            dq.append(fold(mm_tn(sg, k[tokens, lanes]), masks32[g]))
            dk.append(mm(sg, spread(q[tokens, lanes], masks16[g])))
            dv.append(mm(p.astype(BF), many_grad))
        return [jnp.concatenate(t, axis=1) for t in (dq, dk, dv)]

    pieces = [
        attention_back(cprobs, w, cq, ck, cv, c_mixed_grad, COARSE_GROUPS, c_masks16, c_masks32)
        for w in range(2)
    ]
    c_packed = [
        jnp.concatenate([piece[i] for piece in pieces], axis=0).astype(BF) for i in range(3)
    ]
    rolled = mm_nt(c_packed[0], cw[0]) + mm_nt(c_packed[1], cw[1]) + mm_nt(c_packed[2], cw[2])
    bundles[0].step()
    grad_residual = (
        grad_next.astype(F32)
        + norm_back(rolled.astype(BF).astype(F32), c_unit, c_inverse, c_gain)
    ).astype(BF)
    norm_grad = mm_nt(grad_residual, mweight[...]).astype(BF).astype(F32)
    merged_grad = norm_back(norm_grad, m_unit, m_inverse, m_gain)
    for i, row in enumerate(unpaired([merged_grad[:, 192 * t : 192 * t + 192] for t in range(4)])):
        grad_back[8 + i, pl.ds(16, 32)] = row.astype(BF)
    grads = [
        net.start(
            grad_back.at[pl.ds(16, 8), pl.ds(16, 32)], grad_back.at[pl.ds(0, 8), pl.ds(16, 32)],
            net.near(1, 0),
        ),
        net.start(
            grad_back.at[pl.ds(8, 16), pl.ds(32, 16)], grad_back.at[pl.ds(8, 16), pl.ds(0, 16)],
            net.near(0, 1),
        ),
        net.start(
            grad_back.at[pl.ds(16, 8), pl.ds(32, 16)], grad_back.at[pl.ds(0, 8), pl.ds(0, 16)],
            net.near(1, 1),
        ),
    ]
    for t in range(3):
        g_part = mm_tn(n3, c_packed[t])
        for j in range(3):
            works[1][0][pl.ds(72 * t + 24 * j, 24)] = units(
                g_part[:, 128 * j : 128 * j + 128].astype(BF)
            )
    works[1][0][pl.ds(216, 8)] = jnp.zeros((8, 16, 128), BF)
    bundles[1].step()
    g_merge = mm_tn(n2, grad_residual)
    for j in range(3):
        works[2][0][pl.ds(48 * j, 48)] = units(g_merge[:, 128 * j : 128 * j + 128].astype(BF))
    works[2][0][pl.ds(144, 16)] = jnp.zeros((16, 16, 128), BF)
    bundles[2].step()
    bundles[0].step()
    bundles[1].step()

    for copy in grads:
        copy.wait_recv()
    pick = select(32, 48, lambda x: x)
    x = lax.broadcasted_iota(jnp.int32, (32, 48), 0)
    u = lax.broadcasted_iota(jnp.int32, (32, 48), 1)
    pick = jnp.where(folded_place(x + (16 - d1)) == u, 1.0, 0.0).astype(BF)
    block = grad_back[pl.ds(8 - d0, 16)]
    f_grad = to_windows([mm(pick, block[i]) for i in range(16)], 32).astype(BF)
    f_mixed_grad = mm_nt(f_grad, fproj[...]).astype(BF)
    g_fproj = mm_tn(f_mixed, f_grad)
    bundles[2].step()
    pieces = []
    for w in range(8):
        pieces.append(
            attention_back(fprobs, w, fq, fk, fv, f_mixed_grad, FINE_GROUPS, f_masks16, f_masks32)
        )
    g_parts = [
        mm_tn(n1, jnp.concatenate([piece[i] for piece in pieces], axis=0).astype(BF))
        for i in range(3)
    ]
    g_parts.append(g_fproj)
    for t in range(4):
        works[3][0][pl.ds(12 * t, 12)] = units(g_parts[t][:, :128].astype(BF))
    for t in (0, 2):
        tails = jnp.concatenate([g_parts[t][:, 128:], g_parts[t + 1][:, 128:]], axis=1)
        works[3][0][pl.ds(48 + 6 * t, 12)] = units(tails.astype(BF))
    works[3][0][pl.ds(72, 24)] = jnp.zeros((24, 16, 128), BF)
    bundles[3].step()

    for copy in back:
        copy.wait_recv()
    pick = jnp.where(folded_place(x + (16 - b1)) == u, 1.0, 0.0).astype(BF)
    block = head_back[pl.ds(16 - b0, 16)]
    for i in range(16):
        pred[i] = mm(pick, block[i]).astype(BF)

    while any(bundle.stage < 8 for bundle in bundles):
        for bundle in bundles:
            if bundle.stage < 8:
                bundle.step()
    for copy in net.copies:
        copy.wait_send()


N_COPIES = 8 + 3 + 3 + 3 + 3 + 4 * 17


def unpack(r0, r1, r2, r3, pred_in, pred, fq, fp, me, cq, cp, he):
    pred[0] = pred_in[...]

    def take(ref, at, count):
        return ref[pl.ds(at, count)].reshape(count * 16, 128).astype(F32)

    for j in range(6):
        he[:, pl.ds(128 * j, 128)] = take(r0, 24 * j, 24)
    for j in range(3):
        cp[:, pl.ds(128 * j, 128)] = take(r0, 144 + 24 * j, 24)
        me[:, pl.ds(128 * j, 128)] = take(r2, 48 * j, 48)
    for j in range(9):
        cq[:, pl.ds(128 * j, 128)] = take(r1, 24 * j, 24)
    parts = [take(r3, 12 * t, 12) for t in range(4)]
    tails = [take(r3, 48 + 12 * t, 12) for t in range(2)]
    fq[...] = jnp.concatenate(
        [parts[0], tails[0][:, :64], parts[1], tails[0][:, 64:], parts[2], tails[1][:, :64]], axis=1
    )
    fp[...] = jnp.concatenate([parts[3], tails[1][:, 64:]], axis=1)


def on_device(
    latents, actions, action_table, offsets, fine_gain, fine_qkv, fine_bias, fine_proj, merge_gain,
    merge_weight, coarse_gain, coarse_qkv, coarse_bias, coarse_proj, head_weight, cotangent,
):
    smem = pl.BlockSpec(memory_space=pltpu.SMEM)
    vmem = pl.BlockSpec(memory_space=pltpu.VMEM)
    anywhere = pl.BlockSpec(memory_space=pl.ANY)
    scratch = [
        pltpu.VMEM((40, 64, 192), BF),
        pltpu.VMEM((32, 48, 192), BF),
        pltpu.VMEM((24, 48, 192), BF),
        pltpu.VMEM((32, 48, 192), BF),
        pltpu.VMEM((24, 48, 192), BF),
        pltpu.VMEM((8, 64, 384), F32),
        pltpu.VMEM((2, 64, 768), F32),
    ]
    for n in UNITS:
        for shape in ((n,), (n // 2,), (3, n // 8), (n // 2,), (3, n // 32), (n // 8,), (4, n // 32)):
            scratch.append(pltpu.VMEM(shape + (16, 128), BF))
    scratch += [
        pltpu.SemaphoreType.DMA((N_COPIES,)),
        pltpu.SemaphoreType.DMA((N_COPIES,)),
        pltpu.SemaphoreType.DMA((2,)),
    ]
    pred, *results = pl.pallas_call(
        body,
        out_shape=[jax.ShapeDtypeStruct((16, 32, 192), BF)]
        + [jax.ShapeDtypeStruct((n, 16, 128), BF) for n in UNITS],
        in_specs=[smem, smem] + [vmem] * 12 + [anywhere] * 2,
        out_specs=[vmem] * 5,
        scratch_shapes=scratch,
        compiler_params=pltpu.CompilerParams(
            collective_id=0, has_side_effects=True, vmem_limit_bytes=48 * 1024 * 1024
        ),
        name="block_pair",
    )(
        offsets, actions, action_table, fine_gain, fine_qkv, fine_bias, fine_proj, merge_gain,
        merge_weight, coarse_gain, coarse_qkv, coarse_bias, coarse_proj, head_weight, latents,
        cotangent,
    )
    shapes = ((192, 576), (192, 192), (768, 384), (384, 1152), (384, 384), (384, 768))
    return tuple(
        pl.pallas_call(
            unpack,
            out_shape=[jax.ShapeDtypeStruct((1, 16, 32, 192), BF)]
            + [jax.ShapeDtypeStruct(s, F32) for s in shapes],
            in_specs=[vmem] * 5,
            out_specs=[vmem] * 7,
            compiler_params=pltpu.CompilerParams(vmem_limit_bytes=48 * 1024 * 1024),
            name="unpack",
        )(*results, pred)
    )


def solution(mesh):
    split = P(None, "rows", "cols", None)
    return jax.shard_map(
        on_device,
        mesh=mesh,
        in_specs=(split,) + (P(),) * 14 + (split,),
        out_specs=(split,) + (P(),) * 6,
        check_vma=False,
    )
```

profile of v0, /device:TPU:1, one launch (start us, length us, event | category | flops | bytes accessed | tf_op | source)
XLA Modules:
  0.0 119.0 jit_solution(14474078953749939754)
XLA Ops:
  0.6 1.0 copy.23.table
  1.6 0.0 copy-start.1
  1.6 1.2 copy-done.1
  2.8 0.0 copy-start.2
  2.8 1.1 copy-done.2
  3.9 0.0 copy-start.3
  3.9 1.1 copy-done.3
  4.9 0.0 copy-start.4
  4.9 1.0 copy-done.4
  5.9 0.0 copy-start.5
  5.9 1.0 copy-done.5
  6.9 0.0 copy-start.6
  6.9 0.9 copy-done.6
  7.8 0.0 copy-start.7
  7.8 0.9 copy-done.7
  8.8 0.0 copy-start.8
  8.8 0.9 copy-done.8
  9.7 0.0 copy-start.9
  9.7 0.9 copy-done.9
  10.7 0.0 copy-start.10
  10.7 0.9 copy-done.10
  11.6 0.7 copy-done.11
  12.2 0.0 copy-start.12
  12.2 0.7 copy-done.12
  12.9 0.0 copy-start.13
  12.9 0.7 copy-done.13
  13.6 0.7 copy-done.14
  14.3 0.7 copy-done.15
  14.9 100.3 %block_pair.1 = (bf16[16,32,192]{2,1,0:T(8,128)(2,1)S(1)}, bf16[224,16,128]{2,1,0:T(8,128)(2,1)S(1)}, bf16[224,16,128]{2,1,0:T(8,128)(2,1)}, bf16[160,16,128]{2,1,0:T(8,128)(2,1)S(1)}, bf16[96,16,128]{2,1,0:T(8,128)(2,1)S(1)}) custom-call(s32[2,2]{1,0:T(2,128)S(1)} %copy-done.13, s32[1,16]{1,0:T(1,128)S(1)} %copy-done.15, bf16[256,192]{1,0:T(8,128)(2,1)S(1)} %copy.23.table, ...), custom_call_target="tpu_custom_call" | custom-call | tf_op jit(solution)/shard_map/block_pair/pallas_call | solution.py:658
  115.2 0.0 copy-start
  115.2 1.2 copy-done
  116.4 2.6 %unpack.1 = (bf16[1,16,32,192]{3,2,1,0:T(8,128)(2,1)}, f32[192,576]{1,0:T(8,128)}, f32[192,192]{1,0:T(8,128)}, f32[768,384]{1,0:T(8,128)}, f32[384,1152]{1,0:T(8...) custom-call(bf16[224,16,128]{2,1,0:T(8,128)(2,1)S(1)} %get-tuple-element.12.r0, bf16[224,16,128]{2,1,0:T(8,128)(2,1)S(1)} %copy-done, ...), custom_call_target="tpu_custom_call" | custom-call | tf_op jit(solution)/shard_map/unpack/pallas_call | solution.py:676
  (3 shorter events, 0.0 us)
Async XLA Ops:
  1.6 1.2 copy-start.1
  2.8 1.1 copy-start.2
  3.9 1.1 copy-start.3
  4.9 1.0 copy-start.4
  5.9 1.0 copy-start.5
  6.9 0.9 copy-start.6
  7.8 0.9 copy-start.7
  8.8 0.9 copy-start.8
  9.7 0.9 copy-start.9
  10.7 0.9 copy-start.10
  11.6 0.7 copy-start.11
  12.2 0.7 copy-start.12
  12.9 0.7 copy-start.13
  13.6 0.7 copy-start.14
  14.3 0.7 copy-start.15
  115.2 1.2 copy-start
where the time goes:
time: 120 us; the launch traced here: 119 us
  Pallas kernels  103 us (86%)
  local copies, waits for them, and re-layouts  15.4 us (13%)
    pallas_call x1, Pallas kernels, on_device(): pl.pallas_call(body, out_shape=[jax.ShapeDtypeStruct((16, 32, 192), BF)]...  100 us
    unnamed x33, local copies, waits for them, and re-layouts  15.4 us
    pallas_call x1, Pallas kernels, on_device(): pl.pallas_call(unpack, out_shape=[jax.ShapeDtypeStruct((1, 16, 32, 192),...  2.58 us

commit v1 on v0

v1 whole, which is shorter than its diff:
```python
import jax
import jax.numpy as jnp
from jax import lax
from jax.experimental import pallas as pl
from jax.experimental.pallas import tpu as pltpu
from jax.sharding import PartitionSpec as P

MESH = pl.DeviceIdType.MESH
BF = jnp.bfloat16
F32 = jnp.float32
EPS = 1e-05
SCALE = 32 ** (-0.5)
FINE_GROUPS = ((0, 128, 4), (128, 64, 2))
COARSE_GROUPS = ((0, 128, 4), (128, 128, 4), (256, 128, 4))
N_BUNDLES, N_UNITS = 9, 72
ORDERS = (("y", "z", "x"), ("z", "x", "y"), ("x", "y", "z"))


def mm(a, b):
    return lax.dot_general(a, b, (((1,), (0,)), ((), ())), preferred_element_type=F32)


def mm_nt(a, b):
    return lax.dot_general(a, b, (((1,), (1,)), ((), ())), preferred_element_type=F32)


def mm_tn(a, b):
    return lax.dot_general(a, b, (((0,), (0,)), ((), ())), preferred_element_type=F32)


def norm(x):
    centred = x - jnp.mean(x, axis=-1, keepdims=True)
    inverse = lax.rsqrt(jnp.mean(centred * centred, axis=-1, keepdims=True) + EPS)
    return centred * inverse, inverse


def norm_back(upstream, unit, inverse, gain):
    e = upstream * gain
    return inverse * (
        e - jnp.mean(e, axis=-1, keepdims=True) - unit * jnp.mean(e * unit, axis=-1, keepdims=True)
    )


def head_masks(width, heads, dtype):
    lane = lax.broadcasted_iota(jnp.int32, (1, width), 1) // 32
    return [jnp.where(lane == h, 1.0, 0.0).astype(dtype) for h in range(heads)]


def spread(x, masks):
    return jnp.concatenate([x * m for m in masks], axis=0)


def fold(x, masks):
    total = x[:64] * masks[0]
    for h in range(1, len(masks)):
        total = total + x[64 * h : 64 * h + 64] * masks[h]
    return total


def probabilities(q, k, bias, masks):
    s = mm_nt(k, spread(q, masks)) * SCALE + bias
    e = jnp.exp(s - jnp.max(s, axis=0, keepdims=True))
    return e / jnp.sum(e, axis=0, keepdims=True)


def folded_place(u):
    v = u & 15
    return (u - v) + (v & 1) * 8 + (v >> 1)


def true_place(p):
    v = p & 15
    return (p - v) + (v & 7) * 2 + (v >> 3)


def units(x):
    return x.reshape(x.shape[0] // 16, 16, 128)


class Net:
    def __init__(self, send, recv):
        self.r = lax.axis_index("rows")
        self.c = lax.axis_index("cols")
        r, c = self.r, self.c
        self.core = lax.rem(r, 2)
        xlo = lax.rem(r // 2, 2)
        self.y = r // 4
        self.z = c // 2
        xhi = lax.rem(c, 2)
        self.x = xhi * 2 + xlo
        self.low = lax.rem(r, 4)
        self.xhi = xhi
        self.send, self.recv = send, recv
        self.count = 0
        self.copies = []

    def near(self, dr, dc):
        return (lax.rem(self.r + dr + 16, 16), lax.rem(self.c + dc + 8, 8))

    def place(self, axis):
        return {"x": self.x, "y": self.y, "z": self.z}[axis]

    def peer(self, axis, index):
        if axis == "y":
            return (index * 4 + self.low, self.c)
        if axis == "z":
            return (self.r, index * 2 + self.xhi)
        return (self.y * 4 + lax.rem(index, 2) * 2 + self.core, self.z * 2 + index // 2)

    def sibling(self):
        return (self.r + 1 - 2 * self.core, self.c)

    def start(self, source, target, device):
        n = self.count
        self.count += 1
        copy = pltpu.make_async_remote_copy(
            src_ref=source,
            dst_ref=target,
            send_sem=self.send.at[n],
            recv_sem=self.recv.at[n],
            device_id=device,
            device_id_type=MESH,
        )
        copy.start()
        self.copies.append(copy)
        return copy

    def greet(self):
        sem = pltpu.get_barrier_semaphore()
        others = [self.near(a, b) for a in (-1, 0, 1) for b in (-1, 0, 1) if (a, b) != (0, 0)]
        others.append(self.sibling())
        for axis in "xyz":
            others += [self.peer(axis, lax.rem(self.place(axis) + k, 4)) for k in (1, 2, 3)]
        for device in others:
            pl.semaphore_signal(sem, inc=1, device_id=device, device_id_type=MESH)
        self.greeted = len(others)

    def gather(self):
        pl.semaphore_wait(pltpu.get_barrier_semaphore(), self.greeted)


class Reduce:
    def __init__(self, net, order, terms, got_core, got_a, sum_a, got_b, got_c, result):
        self.net, self.order = net, order
        self.terms, self.got_core, self.got_a, self.sum_a = terms, got_core, got_a, sum_a
        self.got_b, self.got_c, self.result = got_b, got_c, result
        self.half, self.part = terms.shape[0] // 2, terms.shape[0] // 8
        self.stage = 0
        self.flight = []

    def step(self):
        getattr(self, "step%d" % self.stage)()
        self.stage += 1

    def arrive(self):
        for copy in self.flight:
            copy.wait_recv()

    def to_peers(self, axis, source, target):
        net = self.net
        me = net.place(axis)
        self.flight = []
        for k in (1, 2, 3):
            to = lax.rem(me + k, 4)
            self.flight.append(net.start(source(to), target(k), net.peer(axis, to)))

    def spread_out(self, total, got, axis):
        me = self.net.place(axis)
        got[pl.ds(me, 1)] = total.astype(BF)[None]
        self.to_peers(axis, lambda to: got.at[me], lambda k: got.at[me])

    def summed(self, got):
        total = got[0].astype(F32)
        for k in (1, 2, 3):
            total = total + got[k].astype(F32)
        return total

    def step0(self):
        net, half = self.net, self.half
        self.flight = [
            net.start(self.terms.at[pl.ds((1 - net.core) * half, half)], self.got_core, net.sibling())
        ]

    def step1(self):
        net, half, part = self.net, self.half, self.part
        self.arrive()
        own = self.terms[pl.ds(net.core * half, half)].astype(F32)
        self.sum_a[...] = (own + self.got_core[...].astype(F32)).astype(BF)
        self.to_peers(
            self.order[0],
            lambda to: self.sum_a.at[pl.ds(to * part, part)],
            lambda k: self.got_a.at[k - 1],
        )

    def step2(self):
        self.arrive()
        me = self.net.place(self.order[0])
        total = self.sum_a[pl.ds(me * self.part, self.part)].astype(F32)
        for k in range(3):
            total = total + self.got_a[k].astype(F32)
        self.spread_out(total, self.got_b, self.order[1])

    def step3(self):
        self.arrive()
        self.spread_out(self.summed(self.got_b), self.got_c, self.order[2])

    def step4(self):
        self.arrive()
        at = self.net.core * self.half + self.net.place(self.order[0]) * self.part
        mine = self.result.at[pl.ds(at, self.part)]
        mine[...] = self.summed(self.got_c).astype(BF)
        self.to_peers(self.order[0], lambda to: mine, lambda k: mine)

    def step5(self):
        self.arrive()
        mine = self.result.at[pl.ds(self.net.core * self.half, self.half)]
        self.flight = [self.net.start(mine, mine, self.net.sibling())]

    def step6(self):
        self.arrive()


def to_map(x, rows, cols):
    wide = cols // 8
    out = []
    for i in range(rows):
        base = (i // 8) * wide
        out.append(
            jnp.concatenate(
                [x[(base + w) * 64 + (i % 8) * 8 :][:8] for w in range(wide)], axis=0
            )
        )
    return out


def to_windows(rows_list, cols):
    wide = cols // 8
    pieces = []
    for wr in range(len(rows_list) // 8):
        for w in range(wide):
            for i in range(8):
                pieces.append(rows_list[wr * 8 + i][8 * w : 8 * w + 8])
    return jnp.concatenate(pieces, axis=0)


def paired(rows_list):
    out = []
    for di in (0, 1):
        for dj in (0, 1):
            out.append(
                jnp.concatenate(
                    [
                        rows_list[2 * i + di][16 * w + 8 * dj :][:8]
                        for w in (0, 1)
                        for i in range(8)
                    ],
                    axis=0,
                )
            )
    return out


def unpaired(parts):
    rows_list = []
    for row in range(16):
        i, di = row // 2, row % 2
        rows_list.append(
            jnp.concatenate(
                [
                    parts[2 * di + dj][64 * w + 8 * i :][:8]
                    for w in (0, 1)
                    for dj in (0, 1)
                ],
                axis=0,
            )
        )
    return rows_list


def packed(x):
    return x.reshape(128, x.shape[-1]).astype(BF).reshape(8, 16, x.shape[-1])


def one_hot(rows_out, cols_in, place):
    x = lax.broadcasted_iota(jnp.int32, (rows_out, cols_in), 0)
    u = lax.broadcasted_iota(jnp.int32, (rows_out, cols_in), 1)
    return jnp.where(place(x) == u, 1.0, 0.0).astype(BF)


def body(*refs):
    (
        offsets, actions, table, fgain, fqkv, fbias, fproj, mgain, mweight, cgain, cqkv, cbias,
        cproj, hweight,
    ) = refs[26:40]
    lat_hbm, cot_hbm = refs[14:16]
    pred_out, *result_outs = refs[16:26]
    (
        lat, lat_left, lat_right, lat_packs, cot, cot_main, cot_next, cot_prev, cot_pack, ahead,
        ahead_side, ahead_pack, head, head_prev, head_next, head_pack, head_rows, back, back_side,
        back_pack, fprobs, cprobs,
    ) = refs[40:62]
    rest = refs[62:]
    works = [rest[6 * g : 6 * g + 6] for g in range(N_BUNDLES)]
    pred, *results = rest[54:64]
    send, recv, local = rest[64:]
    loads = [
        pltpu.make_async_copy(refs[i], refs[26 + i], local.at[2 + i]) for i in range(14)
    ]
    net = Net(send, recv)
    net.greet()
    bundles = [
        Reduce(net, ORDERS[g % 3], *works[g], results[g]) for g in range(N_BUNDLES)
    ]

    def advance(*numbers):
        for g in numbers:
            bundles[g].step()
            if bundles[g].stage == 7:
                copy = pltpu.make_async_copy(results[g], result_outs[g], local.at[17 + g])
                copy.start()
                stores.append(copy)

    stores = []
    own_lat = pltpu.make_async_copy(lat_hbm.at[0], lat.at[pl.ds(8, 16)], local.at[0])
    own_cot = pltpu.make_async_copy(cot_hbm.at[0], cot.at[pl.ds(8, 16)], local.at[1])
    for copy in [own_lat] + loads[:6] + loads[6:] + [own_cot]:
        copy.start()

    own_lat.wait()
    low = lat[pl.ds(8, 16), pl.ds(0, 16)].astype(F32)
    high = lat[pl.ds(8, 16), pl.ds(16, 16)].astype(F32)
    lat_packs[0] = packed(low[:, :8])
    lat_packs[1] = packed(high[:, 8:])
    net.gather()
    lat_halo = []
    for side, (pack, dc) in enumerate(((0, -1), (1, 1))):
        target = lat_right if dc < 0 else lat_left
        for dr, fr, nr, tr in ((0, 0, 8, 4), (-1, 0, 4, 12), (1, 4, 4, 0)):
            lat_halo.append(
                net.start(
                    lat_packs.at[pack, pl.ds(fr, nr)], target.at[pl.ds(tr, nr)], net.near(dr, dc)
                )
            )
    for dr, fr, tr in ((-1, 0, 24), (1, 8, 0)):
        lat_halo.append(
            net.start(lat_hbm.at[0, pl.ds(fr, 8)], lat.at[pl.ds(tr, 8)], net.near(dr, 0))
        )

    for copy in loads:
        copy.wait()
    a0, a1 = offsets[0, 0], offsets[0, 1]
    b0, b1 = 2 * offsets[1, 0], 2 * offsets[1, 1]
    d0, d1 = lax.rem(b0 - a0 + 8, 8), lax.rem(b1 - a1 + 8, 8)
    s0, s1 = lax.rem(b0 - d0 + 8, 16) - 8, lax.rem(b1 - d1 + 8, 16) - 8
    t0, t1 = s0 + d0, s1 + d1
    code = lax.broadcasted_iota(jnp.int32, (8, 256), 1)
    counts = jnp.zeros((8, 256), F32)
    for j in range(16):
        counts = counts + jnp.where(code == actions[0, j], 1.0, 0.0)
    condition = mm_nt(counts.astype(BF), table[...])[:1] * (1.0 / 16.0)
    f_masks16 = [head_masks(w, h, BF) for _, w, h in FINE_GROUPS]
    f_masks32 = [head_masks(w, h, F32) for _, w, h in FINE_GROUPS]
    c_masks16 = [head_masks(w, h, BF) for _, w, h in COARSE_GROUPS]
    c_masks32 = [head_masks(w, h, F32) for _, w, h in COARSE_GROUPS]
    fb = fbias[...].reshape(384, 64).T
    cb = cbias[...].reshape(768, 64).T
    fw = [fqkv[:, 192 * i : 192 * i + 192] for i in range(3)]
    cw = [cqkv[:, 384 * i : 384 * i + 384] for i in range(3)]
    f_gain = fgain[...].reshape(1, 192)
    m_gain = mgain[...].reshape(1, 768)
    c_gain = cgain[...].reshape(1, 384)

    def two_picks(rows_out, cols_in, parity, place):
        return [
            one_hot(rows_out, cols_in, lambda x, p=p: place(x, p))
            for p in (parity * 8, 8 - parity * 8)
        ]

    for copy in lat_halo:
        copy.wait_recv()
    cot_rows = [
        net.start(cot_hbm.at[0], cot.at[pl.ds(24, 16)], net.near(-1, 0)),
        net.start(cot_hbm.at[0, pl.ds(8, 8)], cot.at[pl.ds(0, 8)], net.near(1, 0)),
    ]

    def lat_place(x, p):
        u = x + (s1 + 8)
        return jnp.where(u < 8, 32 + p + u, jnp.where(u < 40, u - 8, 48 + p + u - 40))

    pick = two_picks(32, 64, (8 + s0) & 1, lat_place)
    block = lat[pl.ds(8 + s0, 16)]
    rows_list = []
    for i in range(16):
        pair = (8 + s0 + i) >> 1
        source = jnp.concatenate([block[i], lat_left[pair], lat_right[pair]], axis=0)
        rows_list.append(mm(pick[i % 2], source))
    residual = to_windows(rows_list, 32) + condition
    n1 = (norm(residual)[0] * f_gain).astype(BF)
    fq, fk, fv = (mm(n1, w).astype(BF) for w in fw)
    mixed = []
    for w in range(8):
        tokens = slice(64 * w, 64 * w + 64)
        line = []
        for g, (at, wide, heads) in enumerate(FINE_GROUPS):
            lanes = slice(at, at + wide)
            p = probabilities(
                fq[tokens, lanes], fk[tokens, lanes], fb[:, 64 * (at // 32) :][:, : 64 * heads],
                f_masks16[g],
            )
            fprobs[w, :, pl.ds(64 * (at // 32), 64 * heads)] = p
            line.append(fold(mm_tn(p.astype(BF), fv[tokens, lanes]), f_masks32[g]))
        mixed.append(jnp.concatenate(line, axis=1))
    f_mixed = jnp.concatenate(mixed, axis=0).astype(BF)
    attn = mm(f_mixed, fproj[...]).astype(BF)
    f_next = residual + attn.astype(F32)
    for i, row in enumerate(to_map(f_next, 16, 32)):
        ahead[i] = row.astype(BF)
    for wr in range(2):
        ahead_pack[pl.ds(4 * wr, 4)] = (
            f_next[256 * wr : 256 * wr + 64].astype(BF).reshape(4, 16, 192)
        )
    ahead_halo = [
        net.start(ahead_pack, ahead_side.at[pl.ds(0, 8)], net.near(0, -1)),
        net.start(
            ahead_pack.at[pl.ds(0, 4)], ahead_side.at[pl.ds(8, 4)], net.near(-1, -1)
        ),
        net.start(ahead.at[pl.ds(0, 8)], ahead.at[pl.ds(16, 8)], net.near(-1, 0)),
    ]

    own_cot.wait()
    for copy in cot_rows:
        copy.wait_recv()
    block = cot[pl.ds(8 + t0, 16)]
    cot_main[...] = block
    cot_pack[...] = packed(block[:, 16:].astype(F32)[:, 8:])
    cot_halo = [
        net.start(cot_main.at[:, pl.ds(0, 16)], cot_next, net.near(0, -1)),
        net.start(cot_pack, cot_prev, net.near(0, 1)),
    ]

    def ahead_place(x, p):
        u = true_place(x) + d1
        return jnp.where(u < 32, u, u + p)

    pick = two_picks(32, 48, d0 & 1, ahead_place)
    for copy in ahead_halo:
        copy.wait_recv()
    block = ahead[pl.ds(d0, 16)]
    rows_list = []
    for i in range(16):
        source = jnp.concatenate([block[i], ahead_side[(d0 + i) >> 1]], axis=0)
        rows_list.append(mm(pick[i % 2], source))
    merged = jnp.concatenate(paired(rows_list), axis=1)
    m_unit, m_inverse = norm(merged)
    n2 = (m_unit * m_gain).astype(BF)
    c_residual = mm(n2, mweight[...]).astype(BF).astype(F32)
    c_unit, c_inverse = norm(c_residual)
    n3 = (c_unit * c_gain).astype(BF)
    cq, ck, cv = (mm(n3, w).astype(BF) for w in cw)
    mixed = []
    for w in range(2):
        tokens = slice(64 * w, 64 * w + 64)
        line = []
        for g, (at, wide, heads) in enumerate(COARSE_GROUPS):
            lanes = slice(at, at + wide)
            p = probabilities(
                cq[tokens, lanes], ck[tokens, lanes], cb[:, 64 * (at // 32) :][:, : 64 * heads],
                c_masks16[g],
            )
            cprobs[w, :, pl.ds(64 * (at // 32), 64 * heads)] = p
            line.append(fold(mm_tn(p.astype(BF), cv[tokens, lanes]), c_masks32[g]))
        mixed.append(jnp.concatenate(line, axis=1))
    c_mixed = jnp.concatenate(mixed, axis=0).astype(BF)
    c_attn = mm(c_mixed, cproj[...]).astype(BF)
    c_next = (c_residual + c_attn.astype(F32)).astype(BF)
    head_out = mm(c_next, hweight[...])
    for i, row in enumerate(unpaired([head_out[:, 192 * t : 192 * t + 192] for t in range(4)])):
        head[i] = row.astype(BF)

    for copy in cot_halo:
        copy.wait_recv()

    def cot_place(x, p):
        u = true_place(x) + (t1 + 8)
        return jnp.where(u < 8, 48 + p + u, u - 8)

    pick = two_picks(32, 64, 0, cot_place)
    rows_list = []
    for i in range(16):
        source = jnp.concatenate([cot_main[i], cot_next[i], cot_prev[i // 2]], axis=0)
        rows_list.append(mm(pick[i % 2], source))
    grad_out = jnp.concatenate(paired(rows_list), axis=1).astype(BF)
    grad_next = mm_nt(grad_out, hweight[...]).astype(BF)
    c_mixed_grad = mm_nt(grad_next, cproj[...]).astype(BF)

    g_head = mm_tn(c_next, grad_out)
    for j in range(6):
        works[j // 3][0][pl.ds(24 * (j % 3), 24)] = units(
            g_head[:, 128 * j : 128 * j + 128].astype(BF)
        )
    g_cproj = mm_tn(c_mixed, grad_next)
    for j in range(3):
        works[2][0][pl.ds(24 * j, 24)] = units(g_cproj[:, 128 * j : 128 * j + 128].astype(BF))
    advance(0, 1, 2)

    def attention_back(probs, w, q, k, v, mixed_grad, groups, masks16, masks32):
        tokens = slice(64 * w, 64 * w + 64)
        dq, dk, dv = [], [], []
        for g, (at, wide, heads) in enumerate(groups):
            lanes = slice(at, at + wide)
            p = probs[w, :, pl.ds(64 * (at // 32), 64 * heads)]
            many_grad = spread(mixed_grad[tokens, lanes], masks16[g])
            wg = mm_nt(v[tokens, lanes], many_grad).astype(BF).astype(F32)
            sg = (p * (wg - jnp.sum(p * wg, axis=0, keepdims=True)) * SCALE).astype(BF)
            dq.append(fold(mm_tn(sg, k[tokens, lanes]), masks32[g]))
            dk.append(mm(sg, spread(q[tokens, lanes], masks16[g])))
            dv.append(mm(p.astype(BF), many_grad))
        return [jnp.concatenate(t, axis=1) for t in (dq, dk, dv)]

    pieces = [
        attention_back(cprobs, w, cq, ck, cv, c_mixed_grad, COARSE_GROUPS, c_masks16, c_masks32)
        for w in range(2)
    ]
    c_packed = [
        jnp.concatenate([piece[i] for piece in pieces], axis=0).astype(BF) for i in range(3)
    ]
    rolled = mm_nt(c_packed[0], cw[0]) + mm_nt(c_packed[1], cw[1]) + mm_nt(c_packed[2], cw[2])
    grad_residual = (
        grad_next.astype(F32)
        + norm_back(rolled.astype(BF).astype(F32), c_unit, c_inverse, c_gain)
    ).astype(BF)
    norm_grad = mm_nt(grad_residual, mweight[...]).astype(BF).astype(F32)
    merged_grad = norm_back(norm_grad, m_unit, m_inverse, m_gain)
    rows_list = [
        row.astype(BF)
        for row in unpaired([merged_grad[:, 192 * t : 192 * t + 192] for t in range(4)])
    ]
    last = one_hot(16, 64, lambda x: (x >> 3) * 32 + folded_place(24 + (x & 7)))
    for i in range(8):
        both = jnp.concatenate(rows_list[2 * i : 2 * i + 2], axis=0)
        back[8 + 2 * i], back[9 + 2 * i] = rows_list[2 * i], rows_list[2 * i + 1]
        back_pack[i] = mm(last, both).astype(BF)
    back_halo = [
        net.start(back_pack, back_side.at[pl.ds(4, 8)], net.near(0, 1)),
        net.start(back_pack.at[pl.ds(4, 4)], back_side.at[pl.ds(0, 4)], net.near(1, 1)),
        net.start(back.at[pl.ds(16, 8)], back.at[pl.ds(0, 8)], net.near(1, 0)),
    ]
    advance(0, 1, 2)
    for t in range(3):
        g_part = mm_tn(n3, c_packed[t])
        for j in range(3):
            works[3 + t][0][pl.ds(24 * j, 24)] = units(
                g_part[:, 128 * j : 128 * j + 128].astype(BF)
            )
    advance(3, 4, 5)
    g_merge = mm_tn(n2, grad_residual)
    for t in range(2):
        for j in range(3):
            works[6 + t][0][pl.ds(24 * j, 24)] = units(
                g_merge[384 * t : 384 * t + 384, 128 * j : 128 * j + 128].astype(BF)
            )
    advance(6, 7)
    advance(3, 4, 5)
    first = one_hot(16, 64, lambda x: (x >> 3) * 32 + folded_place(x & 7))
    for i in range(8):
        both = jnp.concatenate([head[2 * i], head[2 * i + 1]], axis=0)
        head_pack[i] = mm(first, both).astype(BF)

    def back_place(x, p):
        u = x + (8 - d1)
        return jnp.where(u < 8, 32 + p + u, folded_place(u - 8))

    pick = two_picks(32, 48, d0 & 1, back_place)
    for copy in back_halo:
        copy.wait_recv()
    advance(6, 7)
    head_halo = [
        net.start(head.at[:, pl.ds(16, 16)], head_prev, net.near(0, 1)),
        net.start(head_pack, head_next, net.near(0, -1)),
    ]

    def turn_rows():
        for copy in head_halo:
            copy.wait_recv()
        pick = two_picks(32, 64, 0, head_place)
        for i in range(16):
            source = jnp.concatenate([head[i], head_prev[i], head_next[i // 2]], axis=0)
            head_rows[16 + i] = mm(pick[i % 2], source).astype(BF)
        return [
            net.start(head_rows.at[pl.ds(16, 16)], head_rows.at[pl.ds(0, 16)], net.near(1, 0)),
            net.start(head_rows.at[pl.ds(16, 8)], head_rows.at[pl.ds(32, 8)], net.near(-1, 0)),
        ]

    def head_place(x, p):
        u = x + (16 - t1)
        return jnp.where(
            u < 16, 32 + folded_place(u), jnp.where(u < 48, folded_place(u - 16), u + p)
        )

    block = back[pl.ds(8 - d0, 16)]
    rows_list = []
    for i in range(16):
        source = jnp.concatenate([block[i], back_side[(8 - d0 + i) >> 1]], axis=0)
        rows_list.append(mm(pick[i % 2], source))
    f_grad = to_windows(rows_list, 32).astype(BF)
    f_mixed_grad = mm_nt(f_grad, fproj[...]).astype(BF)
    g_fproj = mm_tn(f_mixed, f_grad)
    pieces = []
    for w in range(8):
        pieces.append(
            attention_back(fprobs, w, fq, fk, fv, f_mixed_grad, FINE_GROUPS, f_masks16, f_masks32)
        )
        if w == 1:
            advance(0, 1, 2)
        if w == 3:
            advance(3, 4, 5, 6, 7)
            rows_halo = turn_rows()
        if w == 5:
            advance(0, 1, 2)
    g_parts = [
        mm_tn(n1, jnp.concatenate([piece[i] for piece in pieces], axis=0).astype(BF))
        for i in range(3)
    ]
    g_parts.append(g_fproj)
    for t in range(4):
        works[8][0][pl.ds(12 * t, 12)] = units(g_parts[t][:, :128].astype(BF))
    for t in (0, 2):
        tails = jnp.concatenate([g_parts[t][:, 128:], g_parts[t + 1][:, 128:]], axis=1)
        works[8][0][pl.ds(48 + 6 * t, 12)] = units(tails.astype(BF))
    advance(8)
    advance(3, 4, 5, 6, 7)
    advance(8)
    advance(0, 1, 2)
    advance(8)
    advance(3, 4, 5, 6, 7)
    advance(0, 1, 2)
    advance(8)
    for copy in rows_halo:
        copy.wait_recv()
    pred[...] = head_rows[pl.ds(16 - t0, 16)]
    stores.append(pltpu.make_async_copy(pred, pred_out, local.at[16]))
    stores[-1].start()
    advance(3, 4, 5, 6, 7)
    advance(8)
    advance(0, 1, 2)
    advance(8)
    advance(3, 4, 5, 6, 7)
    advance(8)
    for copy in stores:
        copy.wait()
    for copy in net.copies:
        copy.wait_send()


N_COPIES = 8 + 4 + 3 + 3 + 4 + 14 * N_BUNDLES


def unpack(*refs):
    pred_in, *heres = refs[:10]
    pred_out, *outs = refs[10:17]
    packs, wides, held, sems = refs[17:26], refs[26:32], refs[32], refs[33]
    fq, fp, me, cq, cp, he = wides
    pass_in = pltpu.make_async_copy(pred_in, held, sems.at[15])
    pass_on = pltpu.make_async_copy(held, pred_out.at[0], sems.at[16])
    loads = [pltpu.make_async_copy(heres[g], packs[g], sems.at[g]) for g in range(9)]
    stores = [pltpu.make_async_copy(wides[i], outs[i], sems.at[9 + i]) for i in range(6)]
    for copy in loads + [pass_in]:
        copy.start()

    def take(g, at, count):
        return packs[g][pl.ds(at, count)].reshape(count * 16, 128).astype(F32)

    for t in range(3):
        loads[3 + t].wait()
        for j in range(3):
            cq[:, pl.ds(384 * t + 128 * j, 128)] = take(3 + t, 24 * j, 24)
    stores[3].start()
    for t in range(2):
        loads[t].wait()
        for j in range(3):
            he[:, pl.ds(384 * t + 128 * j, 128)] = take(t, 24 * j, 24)
    stores[5].start()
    for t in range(2):
        loads[6 + t].wait()
        for j in range(3):
            me[pl.ds(384 * t, 384), pl.ds(128 * j, 128)] = take(6 + t, 24 * j, 24)
    stores[2].start()
    loads[2].wait()
    for j in range(3):
        cp[:, pl.ds(128 * j, 128)] = take(2, 24 * j, 24)
    stores[4].start()
    pass_in.wait()
    pass_on.start()
    loads[8].wait()
    parts = [take(8, 12 * t, 12) for t in range(4)]
    tails = [take(8, 48 + 12 * t, 12) for t in range(2)]
    fq[...] = jnp.concatenate(
        [parts[0], tails[0][:, :64], parts[1], tails[0][:, 64:], parts[2], tails[1][:, :64]], axis=1
    )
    fp[...] = jnp.concatenate([parts[3], tails[1][:, 64:]], axis=1)
    stores[0].start()
    stores[1].start()
    for copy in stores + [pass_on]:
        copy.wait()


def on_device(
    latents, actions, action_table, offsets, fine_gain, fine_qkv, fine_bias, fine_proj, merge_gain,
    merge_weight, coarse_gain, coarse_qkv, coarse_bias, coarse_proj, head_weight, cotangent,
):
    hbm = pl.BlockSpec(memory_space=pltpu.HBM)
    held = (
        offsets, actions, action_table.T, fine_gain, fine_qkv, fine_bias, fine_proj, merge_gain,
        merge_weight, coarse_gain, coarse_qkv, coarse_bias, coarse_proj, head_weight,
    )
    scratch = [pltpu.SMEM(x.shape, x.dtype) for x in held[:2]]
    scratch += [pltpu.VMEM(x.shape, x.dtype) for x in held[2:]]
    scratch += [
        pltpu.VMEM(shape + (192,), BF)
        for shape in (
            (32, 32), (16, 16), (16, 16), (2, 8, 16), (40, 32), (16, 32), (16, 16), (8, 16),
            (8, 16), (24, 32), (12, 16), (8, 16), (16, 32), (16, 16), (8, 16), (8, 16), (40, 32),
            (24, 32), (12, 16), (8, 16),
        )
    ]
    scratch += [
        pltpu.VMEM((8, 64, 384), F32),
        pltpu.VMEM((2, 64, 768), F32),
    ]
    for _ in range(N_BUNDLES):
        for shape in ((72,), (36,), (3, 9), (36,), (4, 9), (4, 9)):
            scratch.append(pltpu.VMEM(shape + (16, 128), BF))
    scratch.append(pltpu.VMEM((16, 32, 192), BF))
    scratch += [pltpu.VMEM((N_UNITS, 16, 128), BF)] * N_BUNDLES
    scratch += [
        pltpu.SemaphoreType.DMA((N_COPIES,)),
        pltpu.SemaphoreType.DMA((N_COPIES,)),
        pltpu.SemaphoreType.DMA((26,)),
    ]
    pred, *results = pl.pallas_call(
        body,
        out_shape=[jax.ShapeDtypeStruct((16, 32, 192), BF)]
        + [jax.ShapeDtypeStruct((N_UNITS, 16, 128), BF)] * N_BUNDLES,
        in_specs=[hbm] * 16,
        out_specs=[hbm] * 10,
        scratch_shapes=scratch,
        compiler_params=pltpu.CompilerParams(
            collective_id=0, has_side_effects=True, vmem_limit_bytes=60 * 1024 * 1024
        ),
        name="block_pair",
    )(*held, latents, cotangent)
    shapes = ((192, 576), (192, 192), (768, 384), (384, 1152), (384, 384), (384, 768))
    return tuple(
        pl.pallas_call(
            unpack,
            out_shape=[jax.ShapeDtypeStruct((1, 16, 32, 192), BF)]
            + [jax.ShapeDtypeStruct(s, F32) for s in shapes],
            in_specs=[hbm] * 10,
            out_specs=[hbm] * 7,
            scratch_shapes=[pltpu.VMEM((N_UNITS, 16, 128), BF)] * N_BUNDLES
            + [pltpu.VMEM(s, F32) for s in shapes]
            + [pltpu.VMEM((16, 32, 192), BF), pltpu.SemaphoreType.DMA((17,))],
            compiler_params=pltpu.CompilerParams(vmem_limit_bytes=60 * 1024 * 1024),
            name="unpack",
        )(pred, *results)
    )


def solution(mesh):
    split = P(None, "rows", "cols", None)
    return jax.shard_map(
        on_device,
        mesh=mesh,
        in_specs=(split,) + (P(),) * 14 + (split,),
        out_specs=(split,) + (P(),) * 6,
        check_vma=False,
    )
```

time: 120 us -> 86.9 us (0.72)
  Pallas kernels: 103 us -> 86.1 us
  local copies, waits for them, and re-layouts: 15.4 us -> 0 us
    pallas_call x1, Pallas kernels: 100 us -> 82 us  [on_device(): pl.pallas_call(body, out_shape=[jax.ShapeDtypeStruct((16, 32, 192), BF)]...]
    unnamed x33 -> x0, local copies, waits for them, and re-layouts: 15.4 us -> none
    pallas_call x1, Pallas kernels: 2.58 us -> 4.06 us  [on_device(): pl.pallas_call(unpack, out_shape=[jax.ShapeDtypeStruct((1, 16, 32, 192),...]
where the time goes in v1:
time: 86.9 us; the launch traced here: 86.7 us
  Pallas kernels  86.1 us (99%)
    pallas_call x1, Pallas kernels, on_device(): pl.pallas_call(body, out_shape=[jax.ShapeDtypeStruct((16, 32, 192), BF)]...  82 us
    pallas_call x1, Pallas kernels, on_device(): pl.pallas_call(unpack, out_shape=[jax.ShapeDtypeStruct((1, 16, 32, 192),...  4.06 us

profile of v1, /device:TPU:1, one launch (start us, length us, event | category | flops | bytes accessed | tf_op | source)
XLA Modules:
  0.0 86.7 jit_solution(1950050222015956944)
XLA Ops:
  0.6 82.0 %block_pair.1 = (bf16[16,32,192]{2,1,0:T(8,128)(2,1)}, bf16[72,16,128]{2,1,0:T(8,128)(2,1)}, bf16[72,16,128]{2,1,0:T(8,128)(2,1)}, bf16[72,16,128]{2,1,0:T(8,128...) custom-call(s32[2,2]{1,0:T(2,128)} %refs_0_.1, ...), custom_call_target="tpu_custom_call" | custom-call | tf_op jit(solution)/shard_map/block_pair/pallas_call | solution.py:740
  82.6 4.1 %unpack.1 = (bf16[1,16,32,192]{3,2,1,0:T(8,128)(2,1)}, f32[192,576]{1,0:T(8,128)}, f32[192,192]{1,0:T(8,128)}, f32[768,384]{1,0:T(8,128)}, f32[384,1152]{1,0:T(8...) custom-call(bf16[16,32,192]{2,1,0:T(8,128)(2,1)} %get-tuple-element.17.refs_0_, ...), custom_call_target="tpu_custom_call" | custom-call | tf_op jit(solution)/shard_map/unpack/pallas_call | solution.py:754

commit v2 on v1

--- a/solution.py
+++ b/solution.py
@@ -12,7 +12,8 @@
 SCALE = 32 ** (-0.5)
 FINE_GROUPS = ((0, 128, 4), (128, 64, 2))
 COARSE_GROUPS = ((0, 128, 4), (128, 128, 4), (256, 128, 4))
-N_BUNDLES, N_UNITS = 9, 72
+UNITS = (72,) * 8 + (24,) * 3
+N_BUNDLES = len(UNITS)
 ORDERS = (("y", "z", "x"), ("z", "x", "y"), ("x", "y", "z"))
 
 
@@ -57,10 +58,59 @@
     return total
 
 
-def probabilities(q, k, bias, masks):
-    s = mm_nt(k, spread(q, masks)) * SCALE + bias
-    e = jnp.exp(s - jnp.max(s, axis=0, keepdims=True))
-    return e / jnp.sum(e, axis=0, keepdims=True)
+def parts_of(groups, x, w):
+    return [x[64 * w : 64 * w + 64, at : at + wide] for at, wide, _ in groups]
+
+
+def lanes_of(groups, x):
+    return [x[:, 2 * at : 2 * at + 64 * heads] for at, _, heads in groups]
+
+
+def attention(count, groups, q, k, v, bias, masks16, masks32):
+    scores = []
+    for w in range(count):
+        line = [
+            mm_nt(kg, spread(qg, m))
+            for qg, kg, m in zip(parts_of(groups, q, w), parts_of(groups, k, w), masks16)
+        ]
+        scores.append(jnp.concatenate(line, axis=1))
+    s = jnp.stack(scores) * SCALE + bias[None]
+    e = jnp.exp(s - jnp.max(s, axis=1, keepdims=True))
+    probs = e * (1.0 / jnp.sum(e, axis=1, keepdims=True))
+    weights = probs.astype(BF)
+    mixed = []
+    for w in range(count):
+        line = [
+            fold(mm_tn(pg, vg), m)
+            for pg, vg, m in zip(lanes_of(groups, weights[w]), parts_of(groups, v, w), masks32)
+        ]
+        mixed.append(jnp.concatenate(line, axis=1))
+    return probs, jnp.concatenate(mixed, axis=0).astype(BF)
+
+
+def attention_back(count, groups, q, k, v, probs, mixed_grad, masks16, masks32, between):
+    grads = []
+    many = []
+    for w in range(count):
+        many.append(
+            [spread(mg, m) for mg, m in zip(parts_of(groups, mixed_grad, w), masks16)]
+        )
+        line = [mm_nt(vg, mg) for vg, mg in zip(parts_of(groups, v, w), many[w])]
+        grads.append(jnp.concatenate(line, axis=1))
+    wg = jnp.stack(grads).astype(BF).astype(F32)
+    sg = (probs * (wg - jnp.sum(probs * wg, axis=1, keepdims=True)) * SCALE).astype(BF)
+    weights = probs.astype(BF)
+    out = [[], [], []]
+    for w in range(count):
+        between(w)
+        scored, weighed = lanes_of(groups, sg[w]), lanes_of(groups, weights[w])
+        qs, ks = parts_of(groups, q, w), parts_of(groups, k, w)
+        dq = [fold(mm_tn(x, kg), m) for x, kg, m in zip(scored, ks, masks32)]
+        dk = [mm(x, spread(qg, m)) for x, qg, m in zip(scored, qs, masks16)]
+        dv = [mm(x, mg) for x, mg in zip(weighed, many[w])]
+        for have, line in zip(out, (dq, dk, dv)):
+            have.append(jnp.concatenate(line, axis=1))
+    return [jnp.concatenate(x, axis=0).astype(BF) for x in out]
 
 
 def folded_place(u):
@@ -100,12 +150,14 @@
     def place(self, axis):
         return {"x": self.x, "y": self.y, "z": self.z}[axis]
 
-    def peer(self, axis, index):
+    def peer(self, axis, index, core=None):
+        core = self.core if core is None else core
+        low = self.low - self.core + core
         if axis == "y":
-            return (index * 4 + self.low, self.c)
+            return (index * 4 + low, self.c)
         if axis == "z":
-            return (self.r, index * 2 + self.xhi)
-        return (self.y * 4 + lax.rem(index, 2) * 2 + self.core, self.z * 2 + index // 2)
+            return (self.y * 4 + low, index * 2 + self.xhi)
+        return (self.y * 4 + lax.rem(index, 2) * 2 + core, self.z * 2 + index // 2)
 
     def sibling(self):
         return (self.r + 1 - 2 * self.core, self.c)
@@ -131,6 +183,10 @@
         others.append(self.sibling())
         for axis in "xyz":
             others += [self.peer(axis, lax.rem(self.place(axis) + k, 4)) for k in (1, 2, 3)]
+            others += [
+                self.peer(axis, lax.rem(self.place(axis) + k, 4), 1 - self.core)
+                for k in (1, 2, 3)
+            ]
         for device in others:
             pl.semaphore_signal(sem, inc=1, device_id=device, device_id_type=MESH)
         self.greeted = len(others)
@@ -218,6 +274,52 @@
 
     def step6(self):
         self.arrive()
+
+
+class Direct(Reduce):
+    def __init__(self, net, order, terms, got_a, got_b, got_c, result):
+        super().__init__(net, order, terms, None, got_a, None, got_b, got_c, result)
+        self.at = (net.core * 4 + net.place(order[0])) * self.part
+
+    def to_eight(self, source, target):
+        net = self.net
+        me = net.place(self.order[0])
+        self.flight = []
+        for k in range(1, 8):
+            to, core = lax.rem(me + k, 4), lax.rem(net.core + k // 4, 2)
+            self.flight.append(
+                net.start(
+                    source((core * 4 + to) * self.part),
+                    target(k - 1),
+                    net.peer(self.order[0], to, core),
+                )
+            )
+
+    def step0(self):
+        self.to_eight(lambda at: self.terms.at[pl.ds(at, self.part)], lambda k: self.got_a.at[k])
+
+    def step1(self):
+        self.arrive()
+        total = self.terms[pl.ds(self.at, self.part)].astype(F32)
+        for k in range(7):
+            total = total + self.got_a[k].astype(F32)
+        self.spread_out(total, self.got_b, self.order[1])
+
+    def step2(self):
+        self.step3()
+
+    def step3(self):
+        if self.stage == 2:
+            Reduce.step3(self)
+        else:
+            self.arrive()
+            mine = self.result.at[pl.ds(self.at, self.part)]
+            mine[...] = self.summed(self.got_c).astype(BF)
+            self.to_eight(lambda at: mine, lambda k: mine)
+
+    def step4(self):
+        self.arrive()
+        self.stage = 6
 
 
 def to_map(x, rows, cols):
@@ -281,6 +383,31 @@
     return x.reshape(128, x.shape[-1]).astype(BF).reshape(8, 16, x.shape[-1])
 
 
+def pack_rows(x):
+    tails = jnp.concatenate([x[:, :16, 128:], x[:, 16:, 128:]], axis=2)
+    return jnp.concatenate([x[:, :, :128], tails], axis=1)
+
+
+def open_rows(x):
+    tails = jnp.concatenate([x[:, 32:, :64], x[:, 32:, 64:]], axis=1)
+    return jnp.concatenate([x[:, :32], tails], axis=2)
+
+
+def pack_tiles(x):
+    m = x.shape[0] // 2
+    x = x.reshape(m, 2, 16, 192)
+    tails = jnp.concatenate([x[:, 0, :, 128:], x[:, 1, :, 128:]], axis=2)
+    return jnp.stack([x[:, 0, :, :128], x[:, 1, :, :128], tails], axis=1).reshape(3 * m, 16, 128)
+
+
+def open_tiles(x):
+    m = x.shape[0] // 3
+    x = x.reshape(m, 3, 16, 128)
+    first = jnp.concatenate([x[:, 0], x[:, 2, :, :64]], axis=2)
+    second = jnp.concatenate([x[:, 1], x[:, 2, :, 64:]], axis=2)
+    return jnp.stack([first, second], axis=1).reshape(2 * m, 16, 192)
+
+
 def one_hot(rows_out, cols_in, place):
     x = lax.broadcasted_iota(jnp.int32, (rows_out, cols_in), 0)
     u = lax.broadcasted_iota(jnp.int32, (rows_out, cols_in), 1)
@@ -291,25 +418,29 @@
     (
         offsets, actions, table, fgain, fqkv, fbias, fproj, mgain, mweight, cgain, cqkv, cbias,
         cproj, hweight,
-    ) = refs[26:40]
+    ) = refs[28:42]
     lat_hbm, cot_hbm = refs[14:16]
-    pred_out, *result_outs = refs[16:26]
+    pred_out, *result_outs = refs[16:28]
     (
-        lat, lat_left, lat_right, lat_packs, cot, cot_main, cot_next, cot_prev, cot_pack, ahead,
-        ahead_side, ahead_pack, head, head_prev, head_next, head_pack, head_rows, back, back_side,
-        back_pack, fprobs, cprobs,
-    ) = refs[40:62]
-    rest = refs[62:]
-    works = [rest[6 * g : 6 * g + 6] for g in range(N_BUNDLES)]
-    pred, *results = rest[54:64]
-    send, recv, local = rest[64:]
+        lat, lat_left, lat_right, cot, ahead, ahead_side, head, head_rows, back, back_side,
+        lat_rows_out, lat_rows_in, lat_out, lat_left_in, lat_right_in, cot_rows_out, cot_rows_in,
+        cot_next_out, cot_next_in, cot_prev_out, cot_prev_in, ahead_rows_out, ahead_rows_in,
+        ahead_out, ahead_in, back_rows_out, back_rows_in, back_out, back_in, head_prev_out,
+        head_prev_in, head_next_out, head_next_in, head_rows_out, head_rows_in, fprobs, cprobs,
+    ) = refs[42:79]
+    rest = refs[79:]
+    works = [rest[6 * g : 6 * g + 6] for g in range(8)]
+    works += [rest[48 + 4 * g : 52 + 4 * g] for g in range(3)]
+    pred, *results = rest[60:72]
+    send, recv, local = rest[72:]
     loads = [
-        pltpu.make_async_copy(refs[i], refs[26 + i], local.at[2 + i]) for i in range(14)
+        pltpu.make_async_copy(refs[i], refs[28 + i], local.at[2 + i]) for i in range(14)
     ]
     net = Net(send, recv)
     net.greet()
     bundles = [
-        Reduce(net, ORDERS[g % 3], *works[g], results[g]) for g in range(N_BUNDLES)
+        (Reduce if g < 8 else Direct)(net, ORDERS[g % 3], *works[g], results[g])
+        for g in range(N_BUNDLES)
     ]
 
     def advance(*numbers):
@@ -329,22 +460,21 @@
     own_lat.wait()
     low = lat[pl.ds(8, 16), pl.ds(0, 16)].astype(F32)
     high = lat[pl.ds(8, 16), pl.ds(16, 16)].astype(F32)
-    lat_packs[0] = packed(low[:, :8])
-    lat_packs[1] = packed(high[:, 8:])
+    lat_out[0] = pack_tiles(packed(low[:, :8]))
+    lat_out[1] = pack_tiles(packed(high[:, 8:]))
+    lat_rows_out[0] = pack_rows(lat[pl.ds(8, 8)])
+    lat_rows_out[1] = pack_rows(lat[pl.ds(16, 8)])
     net.gather()
     lat_halo = []
-    for side, (pack, dc) in enumerate(((0, -1), (1, 1))):
-        target = lat_right if dc < 0 else lat_left
-        for dr, fr, nr, tr in ((0, 0, 8, 4), (-1, 0, 4, 12), (1, 4, 4, 0)):
+    for side, dc, target in ((0, -1, lat_right_in), (1, 1, lat_left_in)):
+        for dr, fr, nr, tr in ((0, 0, 12, 6), (-1, 0, 6, 18), (1, 6, 6, 0)):
             lat_halo.append(
                 net.start(
-                    lat_packs.at[pack, pl.ds(fr, nr)], target.at[pl.ds(tr, nr)], net.near(dr, dc)
+                    lat_out.at[side, pl.ds(fr, nr)], target.at[pl.ds(tr, nr)], net.near(dr, dc)
                 )
             )
-    for dr, fr, tr in ((-1, 0, 24), (1, 8, 0)):
-        lat_halo.append(
-            net.start(lat_hbm.at[0, pl.ds(fr, 8)], lat.at[pl.ds(tr, 8)], net.near(dr, 0))
-        )
+    lat_halo.append(net.start(lat_rows_out.at[0], lat_rows_in.at[1], net.near(-1, 0)))
+    lat_halo.append(net.start(lat_rows_out.at[1], lat_rows_in.at[0], net.near(1, 0)))
 
     for copy in loads:
         copy.wait()
@@ -366,6 +496,8 @@
     cb = cbias[...].reshape(768, 64).T
     fw = [fqkv[:, 192 * i : 192 * i + 192] for i in range(3)]
     cw = [cqkv[:, 384 * i : 384 * i + 384] for i in range(3)]
+    fproj_t, cproj_t, hweight_t = fproj[...].T, cproj[...].T, hweight[...].T
+    cw_t, mweight_t = [w.T for w in cw], mweight[...].T
     f_gain = fgain[...].reshape(1, 192)
     m_gain = mgain[...].reshape(1, 768)
     c_gain = cgain[...].reshape(1, 384)
@@ -376,12 +508,19 @@
             for p in (parity * 8, 8 - parity * 8)
         ]
 
+    own_cot.wait()
+    cot_rows_out[...] = pack_rows(cot[pl.ds(8, 16)])
+
     for copy in lat_halo:
         copy.wait_recv()
     cot_rows = [
-        net.start(cot_hbm.at[0], cot.at[pl.ds(24, 16)], net.near(-1, 0)),
-        net.start(cot_hbm.at[0, pl.ds(8, 8)], cot.at[pl.ds(0, 8)], net.near(1, 0)),
-    ]
+        net.start(cot_rows_out, cot_rows_in.at[pl.ds(8, 16)], net.near(-1, 0)),
+        net.start(cot_rows_out.at[pl.ds(8, 8)], cot_rows_in.at[pl.ds(0, 8)], net.near(1, 0)),
+    ]
+    lat_left[...] = open_tiles(lat_left_in[...])
+    lat_right[...] = open_tiles(lat_right_in[...])
+    lat[pl.ds(0, 8)] = open_rows(lat_rows_in[0])
+    lat[pl.ds(24, 8)] = open_rows(lat_rows_in[1])
 
     def lat_place(x, p):
         u = x + (s1 + 8)
@@ -397,45 +536,31 @@
     residual = to_windows(rows_list, 32) + condition
     n1 = (norm(residual)[0] * f_gain).astype(BF)
     fq, fk, fv = (mm(n1, w).astype(BF) for w in fw)
-    mixed = []
-    for w in range(8):
-        tokens = slice(64 * w, 64 * w + 64)
-        line = []
-        for g, (at, wide, heads) in enumerate(FINE_GROUPS):
-            lanes = slice(at, at + wide)
-            p = probabilities(
-                fq[tokens, lanes], fk[tokens, lanes], fb[:, 64 * (at // 32) :][:, : 64 * heads],
-                f_masks16[g],
-            )
-            fprobs[w, :, pl.ds(64 * (at // 32), 64 * heads)] = p
-            line.append(fold(mm_tn(p.astype(BF), fv[tokens, lanes]), f_masks32[g]))
-        mixed.append(jnp.concatenate(line, axis=1))
-    f_mixed = jnp.concatenate(mixed, axis=0).astype(BF)
+    f_probs, f_mixed = attention(8, FINE_GROUPS, fq, fk, fv, fb, f_masks16, f_masks32)
+    fprobs[...] = f_probs
     attn = mm(f_mixed, fproj[...]).astype(BF)
     f_next = residual + attn.astype(F32)
     for i, row in enumerate(to_map(f_next, 16, 32)):
         ahead[i] = row.astype(BF)
-    for wr in range(2):
-        ahead_pack[pl.ds(4 * wr, 4)] = (
-            f_next[256 * wr : 256 * wr + 64].astype(BF).reshape(4, 16, 192)
-        )
+    edges = [f_next[256 * wr : 256 * wr + 64].astype(BF) for wr in range(2)]
+    ahead_out[...] = pack_tiles(jnp.concatenate(edges, axis=0).reshape(8, 16, 192))
+    ahead_rows_out[...] = pack_rows(ahead[pl.ds(0, 8)])
     ahead_halo = [
-        net.start(ahead_pack, ahead_side.at[pl.ds(0, 8)], net.near(0, -1)),
-        net.start(
-            ahead_pack.at[pl.ds(0, 4)], ahead_side.at[pl.ds(8, 4)], net.near(-1, -1)
-        ),
-        net.start(ahead.at[pl.ds(0, 8)], ahead.at[pl.ds(16, 8)], net.near(-1, 0)),
-    ]
-
-    own_cot.wait()
+        net.start(ahead_out, ahead_in.at[pl.ds(0, 12)], net.near(0, -1)),
+        net.start(ahead_out.at[pl.ds(0, 6)], ahead_in.at[pl.ds(12, 6)], net.near(-1, -1)),
+        net.start(ahead_rows_out, ahead_rows_in, net.near(-1, 0)),
+    ]
+
     for copy in cot_rows:
         copy.wait_recv()
-    block = cot[pl.ds(8 + t0, 16)]
-    cot_main[...] = block
-    cot_pack[...] = packed(block[:, 16:].astype(F32)[:, 8:])
+    cot[pl.ds(0, 8)] = open_rows(cot_rows_in[pl.ds(0, 8)])
+    cot[pl.ds(24, 16)] = open_rows(cot_rows_in[pl.ds(8, 16)])
+    cot_main = cot[pl.ds(8 + t0, 16)]
+    cot_next_out[...] = pack_tiles(cot_main[:, :16])
+    cot_prev_out[...] = pack_tiles(packed(cot_main[:, 16:].astype(F32)[:, 8:]))
     cot_halo = [
-        net.start(cot_main.at[:, pl.ds(0, 16)], cot_next, net.near(0, -1)),
-        net.start(cot_pack, cot_prev, net.near(0, 1)),
+        net.start(cot_next_out, cot_next_in, net.near(0, -1)),
+        net.start(cot_prev_out, cot_prev_in, net.near(0, 1)),
     ]
 
     def ahead_place(x, p):
@@ -445,6 +570,8 @@
     pick = two_picks(32, 48, d0 & 1, ahead_place)
     for copy in ahead_halo:
         copy.wait_recv()
+    ahead_side[...] = open_tiles(ahead_in[...])
+    ahead[pl.ds(16, 8)] = open_rows(ahead_rows_in[...])
     block = ahead[pl.ds(d0, 16)]
     rows_list = []
     for i in range(16):
@@ -457,25 +584,10 @@
     c_unit, c_inverse = norm(c_residual)
     n3 = (c_unit * c_gain).astype(BF)
     cq, ck, cv = (mm(n3, w).astype(BF) for w in cw)
-    mixed = []
-    for w in range(2):
-        tokens = slice(64 * w, 64 * w + 64)
-        line = []
-        for g, (at, wide, heads) in enumerate(COARSE_GROUPS):
-            lanes = slice(at, at + wide)
-            p = probabilities(
-                cq[tokens, lanes], ck[tokens, lanes], cb[:, 64 * (at // 32) :][:, : 64 * heads],
-                c_masks16[g],
-            )
-            cprobs[w, :, pl.ds(64 * (at // 32), 64 * heads)] = p
-            line.append(fold(mm_tn(p.astype(BF), cv[tokens, lanes]), c_masks32[g]))
-        mixed.append(jnp.concatenate(line, axis=1))
-    c_mixed = jnp.concatenate(mixed, axis=0).astype(BF)
+    c_probs, c_mixed = attention(2, COARSE_GROUPS, cq, ck, cv, cb, c_masks16, c_masks32)
+    cprobs[...] = c_probs
     c_attn = mm(c_mixed, cproj[...]).astype(BF)
     c_next = (c_residual + c_attn.astype(F32)).astype(BF)
-    head_out = mm(c_next, hweight[...])
-    for i, row in enumerate(unpaired([head_out[:, 192 * t : 192 * t + 192] for t in range(4)])):
-        head[i] = row.astype(BF)
 
     for copy in cot_halo:
         copy.wait_recv()
@@ -485,13 +597,14 @@
         return jnp.where(u < 8, 48 + p + u, u - 8)
 
     pick = two_picks(32, 64, 0, cot_place)
+    cot_next, cot_prev = open_tiles(cot_next_in[...]), open_tiles(cot_prev_in[...])
     rows_list = []
     for i in range(16):
         source = jnp.concatenate([cot_main[i], cot_next[i], cot_prev[i // 2]], axis=0)
         rows_list.append(mm(pick[i % 2], source))
     grad_out = jnp.concatenate(paired(rows_list), axis=1).astype(BF)
-    grad_next = mm_nt(grad_out, hweight[...]).astype(BF)
-    c_mixed_grad = mm_nt(grad_next, cproj[...]).astype(BF)
+    grad_next = mm(grad_out, hweight_t).astype(BF)
+    c_mixed_grad = mm(grad_next, cproj_t).astype(BF)
 
     g_head = mm_tn(c_next, grad_out)
     for j in range(6):
@@ -503,47 +616,33 @@
         works[2][0][pl.ds(24 * j, 24)] = units(g_cproj[:, 128 * j : 128 * j + 128].astype(BF))
     advance(0, 1, 2)
 
-    def attention_back(probs, w, q, k, v, mixed_grad, groups, masks16, masks32):
-        tokens = slice(64 * w, 64 * w + 64)
-        dq, dk, dv = [], [], []
-        for g, (at, wide, heads) in enumerate(groups):
-            lanes = slice(at, at + wide)
-            p = probs[w, :, pl.ds(64 * (at // 32), 64 * heads)]
-            many_grad = spread(mixed_grad[tokens, lanes], masks16[g])
-            wg = mm_nt(v[tokens, lanes], many_grad).astype(BF).astype(F32)
-            sg = (p * (wg - jnp.sum(p * wg, axis=0, keepdims=True)) * SCALE).astype(BF)
-            dq.append(fold(mm_tn(sg, k[tokens, lanes]), masks32[g]))
-            dk.append(mm(sg, spread(q[tokens, lanes], masks16[g])))
-            dv.append(mm(p.astype(BF), many_grad))
-        return [jnp.concatenate(t, axis=1) for t in (dq, dk, dv)]
-
-    pieces = [
-        attention_back(cprobs, w, cq, ck, cv, c_mixed_grad, COARSE_GROUPS, c_masks16, c_masks32)
-        for w in range(2)
-    ]
-    c_packed = [
-        jnp.concatenate([piece[i] for piece in pieces], axis=0).astype(BF) for i in range(3)
-    ]
-    rolled = mm_nt(c_packed[0], cw[0]) + mm_nt(c_packed[1], cw[1]) + mm_nt(c_packed[2], cw[2])
+    c_packed = attention_back(
+        2, COARSE_GROUPS, cq, ck, cv, cprobs[...], c_mixed_grad, c_masks16, c_masks32,
+        lambda w: None,
+    )
+    rolled = mm(c_packed[0], cw_t[0]) + mm(c_packed[1], cw_t[1]) + mm(c_packed[2], cw_t[2])
     grad_residual = (
         grad_next.astype(F32)
         + norm_back(rolled.astype(BF).astype(F32), c_unit, c_inverse, c_gain)
     ).astype(BF)
-    norm_grad = mm_nt(grad_residual, mweight[...]).astype(BF).astype(F32)
+    norm_grad = mm(grad_residual, mweight_t).astype(BF).astype(F32)
     merged_grad = norm_back(norm_grad, m_unit, m_inverse, m_gain)
     rows_list = [
         row.astype(BF)
         for row in unpaired([merged_grad[:, 192 * t : 192 * t + 192] for t in range(4)])
     ]
     last = one_hot(16, 64, lambda x: (x >> 3) * 32 + folded_place(24 + (x & 7)))
+    edges = []
     for i in range(8):
         both = jnp.concatenate(rows_list[2 * i : 2 * i + 2], axis=0)
         back[8 + 2 * i], back[9 + 2 * i] = rows_list[2 * i], rows_list[2 * i + 1]
-        back_pack[i] = mm(last, both).astype(BF)
+        edges.append(mm(last, both).astype(BF))
+    back_out[...] = pack_tiles(jnp.stack(edges))
+    back_rows_out[...] = pack_rows(jnp.stack(rows_list[8:]))
     back_halo = [
-        net.start(back_pack, back_side.at[pl.ds(4, 8)], net.near(0, 1)),
-        net.start(back_pack.at[pl.ds(4, 4)], back_side.at[pl.ds(0, 4)], net.near(1, 1)),
-        net.start(back.at[pl.ds(16, 8)], back.at[pl.ds(0, 8)], net.near(1, 0)),
+        net.start(back_out, back_in.at[pl.ds(6, 12)], net.near(0, 1)),
+        net.start(back_out.at[pl.ds(6, 6)], back_in.at[pl.ds(0, 6)], net.near(1, 1)),
+        net.start(back_rows_out, back_rows_in, net.near(1, 0)),
     ]
     advance(0, 1, 2)
     for t in range(3):
@@ -561,10 +660,16 @@
             )
     advance(6, 7)
     advance(3, 4, 5)
+    head_out = mm(c_next, hweight[...])
+    for i, row in enumerate(unpaired([head_out[:, 192 * t : 192 * t + 192] for t in range(4)])):
+        head[i] = row.astype(BF)
     first = one_hot(16, 64, lambda x: (x >> 3) * 32 + folded_place(x & 7))
+    edges = []
     for i in range(8):
         both = jnp.concatenate([head[2 * i], head[2 * i + 1]], axis=0)
-        head_pack[i] = mm(first, both).astype(BF)
+        edges.append(mm(first, both).astype(BF))
+    head_next_out[...] = pack_tiles(jnp.stack(edges))
+    head_prev_out[...] = pack_tiles(head[:, pl.ds(16, 16)])
 
     def back_place(x, p):
         u = x + (8 - d1)
@@ -575,20 +680,22 @@
         copy.wait_recv()
     advance(6, 7)
     head_halo = [
-        net.start(head.at[:, pl.ds(16, 16)], head_prev, net.near(0, 1)),
-        net.start(head_pack, head_next, net.near(0, -1)),
+        net.start(head_prev_out, head_prev_in, net.near(0, 1)),
+        net.start(head_next_out, head_next_in, net.near(0, -1)),
     ]
 
     def turn_rows():
         for copy in head_halo:
             copy.wait_recv()
         pick = two_picks(32, 64, 0, head_place)
+        head_prev, head_next = open_tiles(head_prev_in[...]), open_tiles(head_next_in[...])
         for i in range(16):
             source = jnp.concatenate([head[i], head_prev[i], head_next[i // 2]], axis=0)
             head_rows[16 + i] = mm(pick[i % 2], source).astype(BF)
+        head_rows_out[...] = pack_rows(head_rows[pl.ds(16, 16)])
         return [
-            net.start(head_rows.at[pl.ds(16, 16)], head_rows.at[pl.ds(0, 16)], net.near(1, 0)),
-            net.start(head_rows.at[pl.ds(16, 8)], head_rows.at[pl.ds(32, 8)], net.near(-1, 0)),
+            net.start(head_rows_out, head_rows_in.at[pl.ds(0, 16)], net.near(1, 0)),
+            net.start(head_rows_out.at[pl.ds(0, 8)], head_rows_in.at[pl.ds(16, 8)], net.near(-1, 0)),
         ]
 
     def head_place(x, p):
@@ -597,73 +704,73 @@
             u < 16, 32 + folded_place(u), jnp.where(u < 48, folded_place(u - 16), u + p)
         )
 
+    back_side[...] = open_tiles(back_in[...])
+    back[pl.ds(0, 8)] = open_rows(back_rows_in[...])
     block = back[pl.ds(8 - d0, 16)]
     rows_list = []
     for i in range(16):
         source = jnp.concatenate([block[i], back_side[(8 - d0 + i) >> 1]], axis=0)
         rows_list.append(mm(pick[i % 2], source))
     f_grad = to_windows(rows_list, 32).astype(BF)
-    f_mixed_grad = mm_nt(f_grad, fproj[...]).astype(BF)
+    f_mixed_grad = mm(f_grad, fproj_t).astype(BF)
     g_fproj = mm_tn(f_mixed, f_grad)
-    pieces = []
-    for w in range(8):
-        pieces.append(
-            attention_back(fprobs, w, fq, fk, fv, f_mixed_grad, FINE_GROUPS, f_masks16, f_masks32)
-        )
-        if w == 1:
+
+    def between(w):
+        if w == 0:
             advance(0, 1, 2)
         if w == 3:
             advance(3, 4, 5, 6, 7)
-            rows_halo = turn_rows()
-        if w == 5:
+        if w == 6:
             advance(0, 1, 2)
-    g_parts = [
-        mm_tn(n1, jnp.concatenate([piece[i] for piece in pieces], axis=0).astype(BF))
-        for i in range(3)
-    ]
+
+    f_packed = attention_back(
+        8, FINE_GROUPS, fq, fk, fv, fprobs[...], f_mixed_grad, f_masks16, f_masks32, between
+    )
+    g_parts = [mm_tn(n1, x) for x in f_packed]
     g_parts.append(g_fproj)
     for t in range(4):
-        works[8][0][pl.ds(12 * t, 12)] = units(g_parts[t][:, :128].astype(BF))
+        works[8 + t // 2][0][pl.ds(12 * (t % 2), 12)] = units(g_parts[t][:, :128].astype(BF))
     for t in (0, 2):
         tails = jnp.concatenate([g_parts[t][:, 128:], g_parts[t + 1][:, 128:]], axis=1)
-        works[8][0][pl.ds(48 + 6 * t, 12)] = units(tails.astype(BF))
-    advance(8)
+        works[10][0][pl.ds(6 * t, 12)] = units(tails.astype(BF))
+    advance(8, 9, 10)
     advance(3, 4, 5, 6, 7)
-    advance(8)
+    advance(8, 9, 10)
     advance(0, 1, 2)
-    advance(8)
+    advance(3, 4, 5, 6, 7)
+    advance(8, 9, 10)
+    rows_halo = turn_rows()
+    advance(0, 1, 2)
+    advance(8, 9, 10)
     advance(3, 4, 5, 6, 7)
     advance(0, 1, 2)
-    advance(8)
     for copy in rows_halo:
         copy.wait_recv()
+    head_rows[pl.ds(0, 16)] = open_rows(head_rows_in[pl.ds(0, 16)])
+    head_rows[pl.ds(32, 8)] = open_rows(head_rows_in[pl.ds(16, 8)])
     pred[...] = head_rows[pl.ds(16 - t0, 16)]
     stores.append(pltpu.make_async_copy(pred, pred_out, local.at[16]))
     stores[-1].start()
     advance(3, 4, 5, 6, 7)
-    advance(8)
-    advance(0, 1, 2)
-    advance(8)
-    advance(3, 4, 5, 6, 7)
-    advance(8)
+    advance(8, 9, 10)
     for copy in stores:
         copy.wait()
     for copy in net.copies:
         copy.wait_send()
 
 
-N_COPIES = 8 + 4 + 3 + 3 + 4 + 14 * N_BUNDLES
+N_COPIES = 8 + 4 + 3 + 3 + 4 + 14 * 8 + 20 * 3
 
 
 def unpack(*refs):
-    pred_in, *heres = refs[:10]
-    pred_out, *outs = refs[10:17]
-    packs, wides, held, sems = refs[17:26], refs[26:32], refs[32], refs[33]
+    pred_in, *heres = refs[:12]
+    pred_out, *outs = refs[12:19]
+    packs, wides, held, sems = refs[19:30], refs[30:36], refs[36], refs[37]
     fq, fp, me, cq, cp, he = wides
-    pass_in = pltpu.make_async_copy(pred_in, held, sems.at[15])
-    pass_on = pltpu.make_async_copy(held, pred_out.at[0], sems.at[16])
-    loads = [pltpu.make_async_copy(heres[g], packs[g], sems.at[g]) for g in range(9)]
-    stores = [pltpu.make_async_copy(wides[i], outs[i], sems.at[9 + i]) for i in range(6)]
+    pass_in = pltpu.make_async_copy(pred_in, held, sems.at[17])
+    pass_on = pltpu.make_async_copy(held, pred_out.at[0], sems.at[18])
+    loads = [pltpu.make_async_copy(heres[g], packs[g], sems.at[g]) for g in range(11)]
+    stores = [pltpu.make_async_copy(wides[i], outs[i], sems.at[11 + i]) for i in range(6)]
     for copy in loads + [pass_in]:
         copy.start()
 
@@ -691,9 +798,10 @@
     stores[4].start()
     pass_in.wait()
     pass_on.start()
-    loads[8].wait()
-    parts = [take(8, 12 * t, 12) for t in range(4)]
-    tails = [take(8, 48 + 12 * t, 12) for t in range(2)]
+    for g in (8, 9, 10):
+        loads[g].wait()
+    parts = [take(8 + t // 2, 12 * (t % 2), 12) for t in range(4)]
+    tails = [take(10, 12 * t, 12) for t in range(2)]
     fq[...] = jnp.concatenate(
         [parts[0], tails[0][:, :64], parts[1], tails[0][:, 64:], parts[2], tails[1][:, :64]], axis=1
     )
@@ -718,31 +826,39 @@
     scratch += [
         pltpu.VMEM(shape + (192,), BF)
         for shape in (
-            (32, 32), (16, 16), (16, 16), (2, 8, 16), (40, 32), (16, 32), (16, 16), (8, 16),
-            (8, 16), (24, 32), (12, 16), (8, 16), (16, 32), (16, 16), (8, 16), (8, 16), (40, 32),
-            (24, 32), (12, 16), (8, 16),
+            (32, 32), (16, 16), (16, 16), (40, 32), (24, 32), (12, 16), (16, 32), (40, 32), (24, 32),
+            (12, 16),
+        )
+    ]
+    scratch += [
+        pltpu.VMEM(shape + (128,), BF)
+        for shape in (
+            (2, 8, 48), (2, 8, 48), (2, 12, 16), (24, 16), (24, 16), (16, 48), (24, 48), (24, 16),
+            (24, 16), (12, 16), (12, 16), (8, 48), (8, 48), (12, 16), (18, 16), (8, 48), (8, 48),
+            (12, 16), (18, 16), (24, 16), (24, 16), (12, 16), (12, 16), (16, 48), (24, 48),
         )
     ]
     scratch += [
         pltpu.VMEM((8, 64, 384), F32),
         pltpu.VMEM((2, 64, 768), F32),
     ]
-    for _ in range(N_BUNDLES):
-        for shape in ((72,), (36,), (3, 9), (36,), (4, 9), (4, 9)):
-            scratch.append(pltpu.VMEM(shape + (16, 128), BF))
+    wide = ((72,), (36,), (3, 9), (36,), (4, 9), (4, 9))
+    narrow = ((24,), (7, 3), (4, 3), (4, 3))
+    for shape in wide * 8 + narrow * 3:
+        scratch.append(pltpu.VMEM(shape + (16, 128), BF))
     scratch.append(pltpu.VMEM((16, 32, 192), BF))
-    scratch += [pltpu.VMEM((N_UNITS, 16, 128), BF)] * N_BUNDLES
+    scratch += [pltpu.VMEM((n, 16, 128), BF) for n in UNITS]
     scratch += [
         pltpu.SemaphoreType.DMA((N_COPIES,)),
         pltpu.SemaphoreType.DMA((N_COPIES,)),
-        pltpu.SemaphoreType.DMA((26,)),
+        pltpu.SemaphoreType.DMA((28,)),
     ]
     pred, *results = pl.pallas_call(
         body,
         out_shape=[jax.ShapeDtypeStruct((16, 32, 192), BF)]
-        + [jax.ShapeDtypeStruct((N_UNITS, 16, 128), BF)] * N_BUNDLES,
+        + [jax.ShapeDtypeStruct((n, 16, 128), BF) for n in UNITS],
         in_specs=[hbm] * 16,
-        out_specs=[hbm] * 10,
+        out_specs=[hbm] * 12,
         scratch_shapes=scratch,
         compiler_params=pltpu.CompilerParams(
             collective_id=0, has_side_effects=True, vmem_limit_bytes=60 * 1024 * 1024
@@ -755,11 +871,11 @@
             unpack,
             out_shape=[jax.ShapeDtypeStruct((1, 16, 32, 192), BF)]
             + [jax.ShapeDtypeStruct(s, F32) for s in shapes],
-            in_specs=[hbm] * 10,
+            in_specs=[hbm] * 12,
             out_specs=[hbm] * 7,
-            scratch_shapes=[pltpu.VMEM((N_UNITS, 16, 128), BF)] * N_BUNDLES
+            scratch_shapes=[pltpu.VMEM((n, 16, 128), BF) for n in UNITS]
             + [pltpu.VMEM(s, F32) for s in shapes]
-            + [pltpu.VMEM((16, 32, 192), BF), pltpu.SemaphoreType.DMA((17,))],
+            + [pltpu.VMEM((16, 32, 192), BF), pltpu.SemaphoreType.DMA((19,))],
             compiler_params=pltpu.CompilerParams(vmem_limit_bytes=60 * 1024 * 1024),
             name="unpack",
         )(pred, *results)

time: 86.9 us -> 74.1 us (0.85)
  Pallas kernels: 86.1 us -> 73.3 us
    pallas_call x1, Pallas kernels: 82 us -> 69.3 us  [on_device(): pl.pallas_call(body, out_shape=[jax.ShapeDtypeStruct((16, 32, 192), BF)]...]
where the time goes in v2:
time: 74.1 us; the launch traced here: 74 us
  Pallas kernels  73.3 us (99%)
    pallas_call x1, Pallas kernels, on_device(): pl.pallas_call(body, out_shape=[jax.ShapeDtypeStruct((16, 32, 192), BF)]...  69.3 us
    pallas_call x1, Pallas kernels, on_device(): pl.pallas_call(unpack, out_shape=[jax.ShapeDtypeStruct((1, 16, 32, 192),...  4.08 us

profile of v2, /device:TPU:1, one launch (start us, length us, event | category | flops | bytes accessed | tf_op | source)
XLA Modules:
  0.0 74.0 jit_solution(181034364407407191)
XLA Ops:
  0.6 69.3 %block_pair.1 = (bf16[16,32,192]{2,1,0:T(8,128)(2,1)}, bf16[72,16,128]{2,1,0:T(8,128)(2,1)}, bf16[72,16,128]{2,1,0:T(8,128)(2,1)}, bf16[72,16,128]{2,1,0:T(8,128...) custom-call(s32[2,2]{1,0:T(2,128)} %refs_0_.1, ...), custom_call_target="tpu_custom_call" | custom-call | tf_op jit(solution)/shard_map/block_pair/pallas_call | solution.py:856
  69.9 4.1 %unpack.1 = (bf16[1,16,32,192]{3,2,1,0:T(8,128)(2,1)}, f32[192,576]{1,0:T(8,128)}, f32[192,192]{1,0:T(8,128)}, f32[768,384]{1,0:T(8,128)}, f32[384,1152]{1,0:T(8...) custom-call(bf16[16,32,192]{2,1,0:T(8,128)(2,1)} %get-tuple-element.19.refs_0_, ...), custom_call_target="tpu_custom_call" | custom-call | tf_op jit(solution)/shard_map/unpack/pallas_call | solution.py:870

commit v3 on v2

--- a/solution.py
+++ b/solution.py
@@ -475,6 +475,13 @@
             )
     lat_halo.append(net.start(lat_rows_out.at[0], lat_rows_in.at[1], net.near(-1, 0)))
     lat_halo.append(net.start(lat_rows_out.at[1], lat_rows_in.at[0], net.near(1, 0)))
+
+    own_cot.wait()
+    cot_rows_out[...] = pack_rows(cot[pl.ds(8, 16)])
+    cot_rows = [
+        net.start(cot_rows_out, cot_rows_in.at[pl.ds(8, 16)], net.near(-1, 0)),
+        net.start(cot_rows_out.at[pl.ds(8, 8)], cot_rows_in.at[pl.ds(0, 8)], net.near(1, 0)),
+    ]
 
     for copy in loads:
         copy.wait()
@@ -508,15 +515,8 @@
             for p in (parity * 8, 8 - parity * 8)
         ]
 
-    own_cot.wait()
-    cot_rows_out[...] = pack_rows(cot[pl.ds(8, 16)])
-
     for copy in lat_halo:
         copy.wait_recv()
-    cot_rows = [
-        net.start(cot_rows_out, cot_rows_in.at[pl.ds(8, 16)], net.near(-1, 0)),
-        net.start(cot_rows_out.at[pl.ds(8, 8)], cot_rows_in.at[pl.ds(0, 8)], net.near(1, 0)),
-    ]
     lat_left[...] = open_tiles(lat_left_in[...])
     lat_right[...] = open_tiles(lat_right_in[...])
     lat[pl.ds(0, 8)] = open_rows(lat_rows_in[0])
@@ -589,6 +589,21 @@
     c_attn = mm(c_mixed, cproj[...]).astype(BF)
     c_next = (c_residual + c_attn.astype(F32)).astype(BF)
 
+    head_out = mm(c_next, hweight[...])
+    for i, row in enumerate(unpaired([head_out[:, 192 * t : 192 * t + 192] for t in range(4)])):
+        head[i] = row.astype(BF)
+    first = one_hot(16, 64, lambda x: (x >> 3) * 32 + folded_place(x & 7))
+    edges = []
+    for i in range(8):
+        both = jnp.concatenate([head[2 * i], head[2 * i + 1]], axis=0)
+        edges.append(mm(first, both).astype(BF))
+    head_next_out[...] = pack_tiles(jnp.stack(edges))
+    head_prev_out[...] = pack_tiles(head[:, pl.ds(16, 16)])
+    head_halo = [
+        net.start(head_prev_out, head_prev_in, net.near(0, 1)),
+        net.start(head_next_out, head_next_in, net.near(0, -1)),
+    ]
+
     for copy in cot_halo:
         copy.wait_recv()
 
@@ -660,30 +675,6 @@
             )
     advance(6, 7)
     advance(3, 4, 5)
-    head_out = mm(c_next, hweight[...])
-    for i, row in enumerate(unpaired([head_out[:, 192 * t : 192 * t + 192] for t in range(4)])):
-        head[i] = row.astype(BF)
-    first = one_hot(16, 64, lambda x: (x >> 3) * 32 + folded_place(x & 7))
-    edges = []
-    for i in range(8):
-        both = jnp.concatenate([head[2 * i], head[2 * i + 1]], axis=0)
-        edges.append(mm(first, both).astype(BF))
-    head_next_out[...] = pack_tiles(jnp.stack(edges))
-    head_prev_out[...] = pack_tiles(head[:, pl.ds(16, 16)])
-
-    def back_place(x, p):
-        u = x + (8 - d1)
-        return jnp.where(u < 8, 32 + p + u, folded_place(u - 8))
-
-    pick = two_picks(32, 48, d0 & 1, back_place)
-    for copy in back_halo:
-        copy.wait_recv()
-    advance(6, 7)
-    head_halo = [
-        net.start(head_prev_out, head_prev_in, net.near(0, 1)),
-        net.start(head_next_out, head_next_in, net.near(0, -1)),
-    ]
-
     def turn_rows():
         for copy in head_halo:
             copy.wait_recv()
@@ -704,6 +695,17 @@
             u < 16, 32 + folded_place(u), jnp.where(u < 48, folded_place(u - 16), u + p)
         )
 
+    rows_halo = turn_rows()
+
+    def back_place(x, p):
+        u = x + (8 - d1)
+        return jnp.where(u < 8, 32 + p + u, folded_place(u - 8))
+
+    pick = two_picks(32, 48, d0 & 1, back_place)
+    for copy in back_halo:
+        copy.wait_recv()
+    advance(6, 7)
+
     back_side[...] = open_tiles(back_in[...])
     back[pl.ds(0, 8)] = open_rows(back_rows_in[...])
     block = back[pl.ds(8 - d0, 16)]
@@ -716,12 +718,10 @@
     g_fproj = mm_tn(f_mixed, f_grad)
 
     def between(w):
-        if w == 0:
+        if w == 2:
             advance(0, 1, 2)
-        if w == 3:
+        if w == 7:
             advance(3, 4, 5, 6, 7)
-        if w == 6:
-            advance(0, 1, 2)
 
     f_packed = attention_back(
         8, FINE_GROUPS, fq, fk, fv, fprobs[...], f_mixed_grad, f_masks16, f_masks32, between
@@ -735,15 +735,9 @@
         works[10][0][pl.ds(6 * t, 12)] = units(tails.astype(BF))
     advance(8, 9, 10)
     advance(3, 4, 5, 6, 7)
-    advance(8, 9, 10)
-    advance(0, 1, 2)
-    advance(3, 4, 5, 6, 7)
-    advance(8, 9, 10)
-    rows_halo = turn_rows()
     advance(0, 1, 2)
     advance(8, 9, 10)
     advance(3, 4, 5, 6, 7)
-    advance(0, 1, 2)
     for copy in rows_halo:
         copy.wait_recv()
     head_rows[pl.ds(0, 16)] = open_rows(head_rows_in[pl.ds(0, 16)])
@@ -751,8 +745,14 @@
     pred[...] = head_rows[pl.ds(16 - t0, 16)]
     stores.append(pltpu.make_async_copy(pred, pred_out, local.at[16]))
     stores[-1].start()
+    advance(8, 9, 10)
+    advance(0, 1, 2)
     advance(3, 4, 5, 6, 7)
     advance(8, 9, 10)
+    advance(0, 1, 2)
+    advance(3, 4, 5, 6, 7)
+    advance(8, 9, 10)
+    advance(0, 1, 2)
     for copy in stores:
         copy.wait()
     for copy in net.copies:
@@ -777,25 +777,25 @@
     def take(g, at, count):
         return packs[g][pl.ds(at, count)].reshape(count * 16, 128).astype(F32)
 
+    for t in range(2):
+        loads[t].wait()
+        for j in range(3):
+            he[:, pl.ds(384 * t + 128 * j, 128)] = take(t, 24 * j, 24)
+    stores[5].start()
+    loads[2].wait()
+    for j in range(3):
+        cp[:, pl.ds(128 * j, 128)] = take(2, 24 * j, 24)
+    stores[4].start()
     for t in range(3):
         loads[3 + t].wait()
         for j in range(3):
             cq[:, pl.ds(384 * t + 128 * j, 128)] = take(3 + t, 24 * j, 24)
     stores[3].start()
     for t in range(2):
-        loads[t].wait()
-        for j in range(3):
-            he[:, pl.ds(384 * t + 128 * j, 128)] = take(t, 24 * j, 24)
-    stores[5].start()
-    for t in range(2):
         loads[6 + t].wait()
         for j in range(3):
             me[pl.ds(384 * t, 384), pl.ds(128 * j, 128)] = take(6 + t, 24 * j, 24)
     stores[2].start()
-    loads[2].wait()
-    for j in range(3):
-        cp[:, pl.ds(128 * j, 128)] = take(2, 24 * j, 24)
-    stores[4].start()
     pass_in.wait()
     pass_on.start()
     for g in (8, 9, 10):

time: 74.1 us -> 70.7 us (0.954)
  Pallas kernels: 73.3 us -> 69.9 us
    pallas_call x1, Pallas kernels: 69.3 us -> 66.1 us  [on_device(): pl.pallas_call(body, out_shape=[jax.ShapeDtypeStruct((16, 32, 192), BF)]...]
where the time goes in v3:
time: 70.7 us; the launch traced here: 70.5 us
  Pallas kernels  69.9 us (99%)
    pallas_call x1, Pallas kernels, on_device(): pl.pallas_call(body, out_shape=[jax.ShapeDtypeStruct((16, 32, 192), BF)]...  66.1 us
    pallas_call x1, Pallas kernels, on_device(): pl.pallas_call(unpack, out_shape=[jax.ShapeDtypeStruct((1, 16, 32, 192),...  3.73 us

profile of v3, /device:TPU:1, one launch (start us, length us, event | category | flops | bytes accessed | tf_op | source)
XLA Modules:
  0.0 70.5 jit_solution(15868022643071722431)
XLA Ops:
  0.6 66.1 %block_pair.1 = (bf16[16,32,192]{2,1,0:T(8,128)(2,1)}, bf16[72,16,128]{2,1,0:T(8,128)(2,1)}, bf16[72,16,128]{2,1,0:T(8,128)(2,1)}, bf16[72,16,128]{2,1,0:T(8,128...) custom-call(s32[2,2]{1,0:T(2,128)} %refs_0_.1, ...), custom_call_target="tpu_custom_call" | custom-call | tf_op jit(solution)/shard_map/block_pair/pallas_call | solution.py:856
  66.8 3.7 %unpack.1 = (bf16[1,16,32,192]{3,2,1,0:T(8,128)(2,1)}, f32[192,576]{1,0:T(8,128)}, f32[192,192]{1,0:T(8,128)}, f32[768,384]{1,0:T(8,128)}, f32[384,1152]{1,0:T(8...) custom-call(bf16[16,32,192]{2,1,0:T(8,128)(2,1)} %get-tuple-element.19.refs_0_, ...), custom_call_target="tpu_custom_call" | custom-call | tf_op jit(solution)/shard_map/unpack/pallas_call | solution.py:870

commit v4 on v3

--- a/solution.py
+++ b/solution.py
@@ -695,6 +695,7 @@
             u < 16, 32 + folded_place(u), jnp.where(u < 48, folded_place(u - 16), u + p)
         )
 
+    advance(6, 7)
     rows_halo = turn_rows()
 
     def back_place(x, p):
@@ -704,7 +705,6 @@
     pick = two_picks(32, 48, d0 & 1, back_place)
     for copy in back_halo:
         copy.wait_recv()
-    advance(6, 7)
 
     back_side[...] = open_tiles(back_in[...])
     back[pl.ds(0, 8)] = open_rows(back_rows_in[...])

time: 70.7 us -> 69.5 us (0.983)
  Pallas kernels: 69.9 us -> 68.7 us
    pallas_call x1, Pallas kernels: 66.1 us -> 65 us  [on_device(): pl.pallas_call(body, out_shape=[jax.ShapeDtypeStruct((16, 32, 192), BF)]...]
where the time goes in v4:
time: 69.5 us; the launch traced here: 69.4 us
  Pallas kernels  68.7 us (99%)
    pallas_call x1, Pallas kernels, on_device(): pl.pallas_call(body, out_shape=[jax.ShapeDtypeStruct((16, 32, 192), BF)]...  65 us
    pallas_call x1, Pallas kernels, on_device(): pl.pallas_call(unpack, out_shape=[jax.ShapeDtypeStruct((1, 16, 32, 192),...  3.73 us

profile of v4, /device:TPU:1, one launch (start us, length us, event | category | flops | bytes accessed | tf_op | source)
XLA Modules:
  0.0 69.4 jit_solution(2290408133060940665)
XLA Ops:
  0.6 65.0 %block_pair.1 = (bf16[16,32,192]{2,1,0:T(8,128)(2,1)}, bf16[72,16,128]{2,1,0:T(8,128)(2,1)}, bf16[72,16,128]{2,1,0:T(8,128)(2,1)}, bf16[72,16,128]{2,1,0:T(8,128...) custom-call(s32[2,2]{1,0:T(2,128)} %refs_0_.1, ...), custom_call_target="tpu_custom_call" | custom-call | tf_op jit(solution)/shard_map/block_pair/pallas_call | solution.py:856
  65.6 3.7 %unpack.1 = (bf16[1,16,32,192]{3,2,1,0:T(8,128)(2,1)}, f32[192,576]{1,0:T(8,128)}, f32[192,192]{1,0:T(8,128)}, f32[768,384]{1,0:T(8,128)}, f32[384,1152]{1,0:T(8...) custom-call(bf16[16,32,192]{2,1,0:T(8,128)(2,1)} %get-tuple-element.19.refs_0_, ...), custom_call_target="tpu_custom_call" | custom-call | tf_op jit(solution)/shard_map/unpack/pallas_call | solution.py:870

commit v5 on v4

--- a/solution.py
+++ b/solution.py
@@ -443,13 +443,25 @@
         for g in range(N_BUNDLES)
     ]
 
+    def store(g, start, count, sem):
+        run = pl.ds(start, count)
+        copy = pltpu.make_async_copy(
+            results[g].at[run], result_outs[g].at[run], local.at[sem]
+        )
+        copy.start()
+        stores.append(copy)
+
     def advance(*numbers):
         for g in numbers:
-            bundles[g].step()
-            if bundles[g].stage == 7:
-                copy = pltpu.make_async_copy(results[g], result_outs[g], local.at[17 + g])
-                copy.start()
-                stores.append(copy)
+            bundle = bundles[g]
+            bundle.step()
+            if g >= 8:
+                if bundle.stage == 7:
+                    store(g, 0, UNITS[g], 17 + g)
+            elif bundle.stage == 6:
+                store(g, net.core * bundle.half, bundle.half, 17 + g)
+            elif bundle.stage == 7:
+                store(g, (1 - net.core) * bundle.half, bundle.half, 28 + g)
 
     stores = []
     own_lat = pltpu.make_async_copy(lat_hbm.at[0], lat.at[pl.ds(8, 16)], local.at[0])
@@ -851,7 +863,7 @@
     scratch += [
         pltpu.SemaphoreType.DMA((N_COPIES,)),
         pltpu.SemaphoreType.DMA((N_COPIES,)),
-        pltpu.SemaphoreType.DMA((28,)),
+        pltpu.SemaphoreType.DMA((36,)),
     ]
     pred, *results = pl.pallas_call(
         body,

time: 69.5 us -> 69.4 us (level)
  no operation moved by 1% of the time
where the time goes in v5:
time: 69.4 us; the launch traced here: 69.2 us
  Pallas kernels  68.6 us (99%)
    pallas_call x1, Pallas kernels, on_device(): pl.pallas_call(body, out_shape=[jax.ShapeDtypeStruct((16, 32, 192), BF)]...  64.9 us
    pallas_call x1, Pallas kernels, on_device(): pl.pallas_call(unpack, out_shape=[jax.ShapeDtypeStruct((1, 16, 32, 192),...  3.73 us

profile of v5, /device:TPU:1, one launch (start us, length us, event | category | flops | bytes accessed | tf_op | source)
XLA Modules:
  0.0 69.2 jit_solution(17981225646917146173)
XLA Ops:
  0.6 64.9 %block_pair.1 = (bf16[16,32,192]{2,1,0:T(8,128)(2,1)}, bf16[72,16,128]{2,1,0:T(8,128)(2,1)}, bf16[72,16,128]{2,1,0:T(8,128)(2,1)}, bf16[72,16,128]{2,1,0:T(8,128...) custom-call(s32[2,2]{1,0:T(2,128)} %refs_0_.1, ...), custom_call_target="tpu_custom_call" | custom-call | tf_op jit(solution)/shard_map/block_pair/pallas_call | solution.py:868
  65.5 3.7 %unpack.1 = (bf16[1,16,32,192]{3,2,1,0:T(8,128)(2,1)}, f32[192,576]{1,0:T(8,128)}, f32[192,192]{1,0:T(8,128)}, f32[768,384]{1,0:T(8,128)}, f32[384,1152]{1,0:T(8...) custom-call(bf16[16,32,192]{2,1,0:T(8,128)(2,1)} %get-tuple-element.19.refs_0_, ...), custom_call_target="tpu_custom_call" | custom-call | tf_op jit(solution)/shard_map/unpack/pallas_call | solution.py:882
